TPU v7x, 128 devices: a whole 4x4x4 slice. The times are simulated.
128 devices in a mesh: blk: 32 (over x, y, core), red: 4 (over z).
Axes of the slice: x: 4, y: 4, z: 4, core: 2. Of those that a mesh axis runs over, the one named last changes fastest.
Arguments:
- amplitudes: bfloat16 [16, 8, 1024, 1024], P('red', None, 'blk'), may hold values from -6 to 6
- dressed: bfloat16 [16, 8, 1024, 1024], P('red', None, 'blk'), may hold values from -0.125 to 0.125
- integrals: bfloat16 [8, 8, 1024, 1024], P(None, None, 'blk', 'red'), may hold values from -8 to 8
- occ_irrep: int32 [200], replicated, may hold values from 0 to 7
- virt_irrep: int32 [1024], replicated, may hold values from 0 to 7
- occ_energy: float32 [200], replicated, may hold values from -2 to -0.3
- virt_energy: float32 [1024], replicated, may hold values from 0.1 to 4
- slab_i: int32 [8], replicated, may hold values from 0 to 199
- slab_j: int32 [8], replicated, may hold values from 0 to 199
- slab_k: int32 [16], P('red'), may hold values from 0 to 199
Outputs:
- updated: float32 [8, 8, 1024, 1024], P(None, None, 'blk', 'red')
Inputs may be any that keep to these rules, and one draw needn't show every extreme that they name: `occ_irrep`: irrep labels of the eight irreps of D2h. `virt_irrep`: irrep labels of the eight irreps of D2h. `slab_i`: indices into the 200 occupied orbitals, repeats allowed. `slab_j`: indices into the 200 occupied orbitals, repeats allowed. `slab_k`: indices into the 200 occupied orbitals, repeats allowed.
All inputs are finite; a program needn't handle non-finite values.
Results may differ from a plain program's by a relative error of at most 0.0003.
Values may be sent and summed in bfloat16 or wider, within the bound.
No kernel may reach another device: no remote copies, remote signals or barrier semaphores. Data moves between devices by JAX's collectives and lax.ppermute only.
A program may use at most 192 MiB of HBM per device.

v0:
```python
import functools

import jax
import jax.numpy as jnp
import numpy as np
from jax import lax
from jax.experimental import pallas as pl
from jax.experimental.pallas import tpu as pltpu
from jax.sharding import PartitionSpec as P

F32 = jnp.float32
BF16 = jnp.bfloat16
I32 = jnp.int32

RING = 4
CORES = 2
WIDES = (192, 160)
PARTS = (64, 48)
STEPS = (1, 3, 2, 0)
LANES = 128


def table_lookup(table, picks):
    hits = picks[:, None] == jnp.arange(table.shape[0], dtype=jnp.int32)[None, :]
    return jnp.sum(jnp.where(hits, table[None, :], jnp.zeros((), table.dtype)), axis=1)


def dense_form(
    amplitudes,
    dressed,
    integrals,
    occ_irrep,
    virt_irrep,
    occ_energy,
    virt_energy,
    slab_i,
    slab_j,
    slab_k,
):
    blk_size = lax.axis_size("blk")
    red_size = lax.axis_size("red")
    k_local, slab_rows, virt_rows, virt_all = amplitudes.shape
    occ_cols = dressed.shape[1]
    cols_kept = virt_all // red_size
    pair_count = slab_rows * occ_cols // blk_size
    own_rows = max(1, pair_count // occ_cols)
    own_cols = min(pair_count, occ_cols)
    owners = np.arange(blk_size)
    first_pair = owners * pair_count
    table_rows = ((first_pair // occ_cols)[:, None] + np.arange(own_rows)[None, :]).reshape(-1)
    table_cols = ((first_pair % occ_cols)[:, None] + np.arange(own_cols)[None, :]).reshape(-1)
    blk_place = lax.axis_index("blk")
    red_place = lax.axis_index("red")
    label_i = table_lookup(occ_irrep, slab_i)
    label_j = table_lookup(occ_irrep, slab_j)
    label_k = table_lookup(occ_irrep, slab_k)
    rows_label = lax.dynamic_slice_in_dim(virt_irrep, blk_place * virt_rows, virt_rows)
    pair_virt = jnp.bitwise_xor(rows_label[:, None], virt_irrep[None, :])
    amp_sym = jnp.bitwise_xor(
        jnp.bitwise_xor(label_k[:, None], label_i[None, :])[:, :, None, None], pair_virt[None, None]
    )
    kept_amp = jnp.where(amp_sym == 0, amplitudes, jnp.zeros((), amplitudes.dtype))
    dre_sym = jnp.bitwise_xor(
        jnp.bitwise_xor(label_k[:, None], label_j[None, :])[:, :, None, None], pair_virt[None, None]
    )
    kept_dre = jnp.where(dre_sym == 0, dressed, jnp.zeros((), dressed.dtype))
    send_amp = jnp.take(kept_amp, table_rows, axis=1).reshape(
        k_local, blk_size, own_rows, virt_rows, virt_all
    )
    send_dre = jnp.take(kept_dre, table_cols, axis=1).reshape(
        k_local, blk_size, own_cols, virt_rows, virt_all
    )
    amp_owner = lax.all_to_all(send_amp, "blk", split_axis=1, concat_axis=3, tiled=True)[:, 0]
    dre_owner = lax.all_to_all(send_dre, "blk", split_axis=1, concat_axis=3, tiled=True)[:, 0]
    partial_cycle = jnp.einsum(
        "kiac,kjcb->ijab", amp_owner, dre_owner, preferred_element_type=jnp.float32
    )
    by_cols = partial_cycle.reshape(pair_count, virt_all, red_size, cols_kept)
    cycle_pairs = lax.all_to_all(by_cols, "red", split_axis=2, concat_axis=2, tiled=True).sum(axis=2)
    cycle_kept = lax.all_to_all(
        cycle_pairs, "blk", split_axis=1, concat_axis=0, tiled=True
    ).reshape(slab_rows, occ_cols, virt_rows, cols_kept)
    energy_i = table_lookup(occ_energy, slab_i)
    energy_j = table_lookup(occ_energy, slab_j)
    energy_a = lax.dynamic_slice_in_dim(virt_energy, blk_place * virt_rows, virt_rows)
    energy_b = lax.dynamic_slice_in_dim(virt_energy, red_place * cols_kept, cols_kept)
    label_b = lax.dynamic_slice_in_dim(virt_irrep, red_place * cols_kept, cols_kept)
    denom = (
        energy_i[:, None, None, None]
        + energy_j[None, :, None, None]
        - energy_a[None, None, :, None]
        - energy_b[None, None, None, :]
    )
    out_virt = jnp.bitwise_xor(rows_label[:, None], label_b[None, :])
    out_sym = jnp.bitwise_xor(
        jnp.bitwise_xor(label_i[:, None], label_j[None, :])[:, :, None, None], out_virt[None, None]
    )
    value = (integrals.astype(jnp.float32) + cycle_kept) / denom
    return jnp.where(out_sym == 0, value, jnp.zeros((), jnp.float32))


def coords():
    blk = lax.axis_index("blk")
    return blk // (RING * CORES), (blk // CORES) % RING, blk % CORES, lax.axis_index("red")


def iota(shape, dim):
    return lax.broadcasted_iota(I32, shape, dim)


def picked_column(row, first, count):
    wide = row.shape[1]
    hit = iota((count, wide), 1) == iota((count, wide), 0) + first
    kept = jnp.where(hit, jnp.broadcast_to(row.astype(F32), (count, wide)), 0.0)
    return jnp.sum(kept, axis=1, keepdims=True).astype(row.dtype)


def one_hot(count, first, row):
    slot = (iota((count, 1), 0) + first).astype(F32).astype(BF16)
    there = jnp.clip(row, -1, 256).astype(F32).astype(BF16)
    return jnp.where(slot == there, jnp.ones((), BF16), jnp.zeros((), BF16))


def rest_hot(groups, group, half, rank):
    share = half // groups
    slot = iota((half, 1), 0) - group * share
    inside = jnp.logical_and(slot >= 0, slot < share)
    slot = jnp.where(inside, slot + half, 512).astype(F32).astype(BF16)
    there = jnp.clip(rank, -1, 256).astype(F32).astype(BF16)
    return jnp.where(slot == there, jnp.ones((), BF16), jnp.zeros((), BF16))


def label_ranks(lv_ref, rank_ref, part_ref, fits_ref):
    wide = lv_ref.shape[1]
    quarter = wide // RING
    tri = (iota((quarter, quarter), 0) < iota((quarter, quarter), 1)).astype(F32).astype(BF16)
    base = jnp.zeros((16, 1), F32)
    most_part = jnp.zeros((1, 1), F32)
    for part in range(RING):
        lanes = slice(part * quarter, (part + 1) * quarter)
        member = (iota((16, quarter), 0) == lv_ref[:, lanes]).astype(F32)
        before = jnp.dot(member.astype(BF16), tri, preferred_element_type=F32)
        part_ref[:, lanes] = jnp.sum(member * before, axis=0, keepdims=True).astype(I32)
        rank_ref[:, lanes] = jnp.sum(member * (before + base), axis=0, keepdims=True).astype(I32)
        count = jnp.sum(member, axis=1, keepdims=True)
        most_part = jnp.maximum(most_part, jnp.max(count))
        base = base + count
    most = jnp.max(most_part)
    whole_most = jnp.max(base)
    fits = jnp.logical_and(whole_most <= WIDES[0], most <= PARTS[0])
    tight = jnp.logical_and(whole_most <= WIDES[1], most <= PARTS[1])
    fits_ref[0] = fits.astype(I32) + tight.astype(I32)


def masked_rows(kept, at, label, own_label, lv, block):
    rows = block.shape[0]
    wanted = jnp.bitwise_xor(own_label, label).astype(F32).astype(BF16)
    kept[at * rows : (at + 1) * rows, :] = jnp.where(wanted == lv, block, jnp.zeros((), BF16))


def pack_dressed_kernel(
    slots,
    occ_ref,
    sj_ref,
    sk_ref,
    lv_ref,
    dre_ref,
    p0,
    p1,
    p2,
    p3,
    rank_ref,
    part_ref,
    fits_ref,
    hot_part,
    own_label,
    kept,
):
    _, y, _, z = coords()
    n = pl.program_id(0)
    n_k, _, rows, wide = dre_ref.shape
    lv = lv_ref[...].astype(F32).astype(BF16)

    @pl.when(n == 0)
    def _():
        label_ranks(lv_ref, rank_ref, part_ref, fits_ref)
        step = (iota((1, wide), 1) // (wide // RING) - z + RING) % RING
        first = jnp.zeros((1, wide), I32)
        for n_step, s in enumerate(STEPS):
            first = jnp.where(step == s, n_step * slots, first)
        place = first + jnp.minimum(part_ref[...], slots - 1)
        hot_part[...] = one_hot(RING * slots, 0, place).T
        own_label[...] = picked_column(lv_ref[...], lax.axis_index("blk") * rows, rows)

    for k in range(n_k):
        lk = occ_ref[sk_ref[n * n_k + k]]
        for d in range(RING):
            for jj in range(CORES):
                j = ((y + d) % RING) * CORES + jj
                label = jnp.bitwise_xor(lk, occ_ref[sj_ref[j]])
                at = (jj * RING + d) * n_k + k
                masked_rows(kept, at, label, own_label[...], lv, dre_ref[k, j])
    count = n_k * rows
    packed = jnp.dot(kept[...], hot_part[...], preferred_element_type=F32)
    for d, out in enumerate((p0, p1, p2, p3)):
        even = packed[d * count : (d + 1) * count]
        odd = packed[(RING + d) * count : (RING + d + 1) * count]
        pieces = []
        for s in range(RING):
            at = slice(s * slots, (s + 1) * slots)
            pieces += [even[:, at], odd[:, at]]
        out[...] = jnp.concatenate(pieces, axis=1).astype(BF16).reshape(out.shape)


def pack_amplitudes_kernel(
    occ_ref,
    si_ref,
    sk_ref,
    lv_ref,
    rank_ref,
    amp_ref,
    pa_ref,
    hot_main,
    hot_rest,
    own_label,
    kept,
):
    n = pl.program_id(0)
    n_k, n_i, rows, wide = amp_ref.shape
    half = hot_main.shape[1]
    groups = hot_rest.shape[0]
    lv = lv_ref[...].astype(F32).astype(BF16)

    @pl.when(n == 0)
    def _():
        rank = rank_ref[...]
        hot_main[...] = one_hot(half, 0, rank).T
        for group in range(groups):
            hot_rest[group] = rest_hot(groups, group, half, rank).T
        own_label[...] = picked_column(lv_ref[...], lax.axis_index("blk") * rows, rows)

    for i in range(n_i):
        for k in range(n_k):
            label = jnp.bitwise_xor(occ_ref[sk_ref[n * n_k + k]], occ_ref[si_ref[i]])
            masked_rows(kept, i * n_k + k, label, own_label[...], lv, amp_ref[k, i])
    main = jnp.dot(kept[...], hot_main[...], preferred_element_type=F32).astype(BF16)
    count = n_i * n_k * rows // groups
    rest = jnp.zeros((count, half), F32)
    for group in range(groups):
        block = kept[group * count : (group + 1) * count]
        rest += jnp.dot(block, hot_rest[group], preferred_element_type=F32)
    main = main.reshape(n_i, n_k, rows, half)
    rest = rest.astype(BF16).reshape(n_i // groups, n_k, rows, half)
    for d in range(RING):
        for k in range(n_k):
            pa_ref[d, k, :n_i] = main[:, k]
            pa_ref[d, k, n_i:] = rest[:, k]


def unpack_kernel(
    occ_ref, si_ref, sk_ref, lv_ref, rank_ref, pa_ref, out_ref, hot, order, labels
):
    x, y, core, _ = coords()
    k = pl.program_id(0)
    n_rest, rows, half = pa_ref.shape[2:]
    groups = hot.shape[0]
    n_i = n_rest * groups // (groups + 1)
    wide = lv_ref.shape[1]

    @pl.when(k == 0)
    def _():
        p = iota((1, wide), 1)
        source = (
            ((x - (p // (4 * rows)) % RING + RING) % RING) * (rows * 8)
            + ((y - (p // rows) % RING + RING) % RING) * (rows * 2)
            + jnp.bitwise_xor(core, p // (wide // 2)) * rows
            + p % rows
        )
        pick = (iota((wide, wide), 0) == source).astype(F32).astype(BF16)
        which = iota((16, wide), 0)
        both = jnp.where(
            which == 0,
            jnp.broadcast_to(lv_ref[...], (16, wide)),
            jnp.broadcast_to(jnp.minimum(rank_ref[...], 255), (16, wide)),
        )
        moved = jnp.dot(both.astype(F32).astype(BF16), pick, preferred_element_type=F32).astype(I32)
        order[...] = moved[0:1].astype(F32).astype(BF16)
        rank = moved[1:2]
        main = one_hot(half, 0, rank)
        for side in range(groups):
            hot[side, :half] = main
            hot[side, half:] = rest_hot(groups, side, half, rank)
        for d in range(RING):
            first = x * (rows * 8) + ((y - d + RING) % RING) * (rows * 2) + core * rows
            labels[d] = picked_column(lv_ref[...], first, rows)

    lk = occ_ref[sk_ref[k]]
    group = n_i // groups
    blocks = [pa_ref.at[(y - d + RING) % RING] for d in range(RING)]
    for side in range(groups):
        pairs = []
        for block in blocks:
            main = block[0, side * group : (side + 1) * group].reshape(group * rows, half)
            rest = block[0, n_i:].reshape(group * rows, half)
            pairs.append(jnp.concatenate([main, rest], axis=1))
        spread = jnp.dot(
            jnp.concatenate(pairs, axis=0), hot[side], preferred_element_type=F32
        )
        for d in range(RING):
            for g in range(group):
                i = side * group + g
                label = jnp.bitwise_xor(lk, occ_ref[si_ref[i]])
                wanted = jnp.bitwise_xor(labels[d], label).astype(F32).astype(BF16)
                at = (d * n_i + i) * rows
                source = (d * group + g) * rows
                out_ref[0, at : at + rows, :] = jnp.where(
                    wanted == order[...],
                    spread[source : source + rows].astype(BF16),
                    jnp.zeros((), BF16),
                )


def folded(value, n_i, rows):
    used = value.shape[1]
    blocks = [value[n * rows : (n + 1) * rows] for n in range(value.shape[0] // rows)]
    if used == LANES:
        return blocks
    hosts = used // (LANES - used)
    held = n_i * hosts // (hosts + 1)
    out = []
    for d in range(len(blocks) // n_i):
        for i in range(held):
            guest = blocks[d * n_i + held + i // hosts]
            at = (i % hosts) * (LANES - used)
            out.append(
                jnp.concatenate([blocks[d * n_i + i], guest[:, at : at + LANES - used]], axis=1)
            )
    return out


def cycle_kernel(
    n_i, slots, first, a_ref, b0, b1, b2, b3, b4, b5, b6, b7, o0, o1, b_all, total
):
    k = pl.program_id(0)
    rows = b0.shape[2]
    depth = b0.shape[0] * rows
    start = first * CORES * slots // LANES * LANES
    for n, b in enumerate((b0, b1, b2, b3, b4, b5, b6, b7)):
        b_all[n * depth : (n + 1) * depth, :] = b[:, 0, :, start : start + 256].reshape(depth, 256)
    term = jnp.dot(a_ref[0], b_all[...], preferred_element_type=F32)

    @pl.when(k == 0)
    def _():
        total[...] = term

    @pl.when(jnp.logical_and(k > 0, k < pl.num_programs(0) - 1))
    def _():
        total[...] += term

    @pl.when(k == pl.num_programs(0) - 1)
    def _():
        full = total[...] + term
        for n, out in enumerate((o0, o1)):
            at = (first + n) * CORES * slots - start
            for m, block in enumerate(folded(full[:, at : at + CORES * slots], n_i, rows)):
                out[m // out.shape[1], m % out.shape[1]] = block


def sum_kernel(o0, o1, o2, o3, s0, s1, s2, s3):
    for d, out in enumerate((s0, s1, s2, s3)):
        out[...] = ((o0[d] + o1[d]) + o2[d]) + o3[d]


def update_kernel(
    slots,
    occ_ref,
    si_ref,
    sj_ref,
    oe_ref,
    lv_ref,
    ve_ref,
    part_ref,
    t0,
    t1,
    t2,
    t3,
    int_ref,
    out_ref,
    hot,
    own_label,
    own_energy,
    three,
):
    _, y, _, z = coords()
    n = pl.program_id(0)
    held, rows, lanes = t0.shape
    n_i, _, _, kept = int_ref.shape
    cols = pl.ds(pl.multiple_of(z * kept, kept), kept)

    @pl.when(n == 0)
    def _():
        slot = iota((lanes, kept), 0)
        part = part_ref[:, cols]
        for jj in range(CORES):
            one = (slot == part + jj * slots).astype(F32).astype(BF16)
            for n in range(3):
                hot[n * lanes : (n + 1) * lanes, jj * kept : (jj + 1) * kept] = one
        first = lax.axis_index("blk") * rows
        own_label[...] = picked_column(lv_ref[...], first, rows)
        own_energy[...] = picked_column(ve_ref[...], first, rows)

    spare = lanes - CORES * slots

    @pl.when(n == 0)
    def _():
        for d, t in enumerate((t0, t1, t2, t3)):
            for i in range(three.shape[0]):
                if i < held:
                    x = t[i]
                else:
                    hosts = CORES * slots // spare
                    first_host = (i - held) * hosts
                    x = jnp.concatenate(
                        [t[first_host + h][:, lanes - spare :] for h in range(hosts)]
                        + [jnp.zeros((rows, spare), F32)],
                        axis=1,
                    )
                top = x.astype(BF16)
                left = x - top.astype(F32)
                mid = left.astype(BF16)
                low = (left - mid.astype(F32)).astype(BF16)
                three[i, d * rows : (d + 1) * rows] = jnp.concatenate([top, mid, low], axis=1)

    label_b = lv_ref[:, cols]
    energy_b = ve_ref[:, cols]
    for e in range(n_i):
        i = n * n_i + e
        cycle = jnp.dot(three[i], hot[...], preferred_element_type=F32)
        label_i = occ_ref[si_ref[i]]
        energy_i = oe_ref[si_ref[i]]
        for d in range(RING):
            for jj in range(CORES):
                j = ((y + d) % RING) * CORES + jj
                label = jnp.bitwise_xor(label_i, occ_ref[sj_ref[j]])
                denom = ((energy_i + oe_ref[sj_ref[j]]) - own_energy[...]) - energy_b
                term = cycle[d * rows : (d + 1) * rows, jj * kept : (jj + 1) * kept]
                value = (int_ref[e, j].astype(F32) + term) / denom
                keep = jnp.bitwise_xor(own_label[...], label) == label_b
                out_ref[e, j] = jnp.where(keep, value, 0.0)


SMEM = pl.BlockSpec(memory_space=pltpu.SMEM)


def whole(shape):
    return pl.BlockSpec(shape, lambda n: (0,) * len(shape))


def cost(flops, moved):
    return pl.CostEstimate(flops=flops, bytes_accessed=moved, transcendentals=0)


def halves(shape, dim):
    block = tuple(size // 2 if at == dim else size for at, size in enumerate(shape))
    return pl.BlockSpec(block, lambda n: tuple(n if at == dim else 0 for at in range(len(shape))))


def pack_dressed(slots, dressed, occ_irrep, virt_irrep, slab_j, slab_k):
    n_k, n_j, rows, wide = dressed.shape
    out = (n_k, rows, RING * CORES * slots)
    row_spec = whole((1, wide))
    row = jax.ShapeDtypeStruct((1, wide), I32)
    *pb, rank, part, fits = pl.pallas_call(
        functools.partial(pack_dressed_kernel, slots),
        grid=(2,),
        out_shape=[jax.ShapeDtypeStruct(out, BF16)] * RING
        + [row, row, jax.ShapeDtypeStruct((1,), I32)],
        in_specs=[SMEM] * 3 + [row_spec, halves(dressed.shape, 0)],
        out_specs=[halves(out, 0)] * RING + [row_spec, row_spec, SMEM],
        scratch_shapes=[
            pltpu.VMEM((wide, RING * slots), BF16),
            pltpu.VMEM((rows, 1), I32),
            pltpu.VMEM((n_k * n_j * rows // 2, wide), BF16),
        ],
        compiler_params=pltpu.CompilerParams(vmem_limit_bytes=32 * 1024 * 1024),
        cost_estimate=cost(2 * n_k * n_j * rows * wide * 256, 10 << 20),
        name="pack_dressed",
    )(occ_irrep, slab_j, slab_k, virt_irrep.reshape(1, wide), dressed)
    return pb, rank, part, fits


def pack_amplitudes(slots, amplitudes, rank, occ_irrep, virt_irrep, slab_i, slab_k):
    n_k, n_i, rows, wide = amplitudes.shape
    half = LANES
    groups = half // (slots - half)
    out = (RING, n_k, n_i + n_i // groups, rows, half)
    row_spec = whole((1, wide))
    return pl.pallas_call(
        pack_amplitudes_kernel,
        grid=(2,),
        out_shape=jax.ShapeDtypeStruct(out, BF16),
        in_specs=[SMEM] * 3 + [row_spec, row_spec, halves(amplitudes.shape, 0)],
        out_specs=halves(out, 1),
        scratch_shapes=[
            pltpu.VMEM((wide, half), BF16),
            pltpu.VMEM((groups, wide, half), BF16),
            pltpu.VMEM((rows, 1), I32),
            pltpu.VMEM((n_k * n_i * rows // 2, wide), BF16),
        ],
        compiler_params=pltpu.CompilerParams(vmem_limit_bytes=32 * 1024 * 1024),
        cost_estimate=cost(2 * n_k * n_i * rows * wide * 256, 10 << 20),
        name="pack_amplitudes",
    )(occ_irrep, slab_i, slab_k, virt_irrep.reshape(1, wide), rank, amplitudes)


def ring_y(d):
    return [
        (8 * x + 2 * y + c, 8 * x + 2 * ((y + d) % RING) + c)
        for x in range(RING)
        for y in range(RING)
        for c in range(CORES)
    ]


def groups_y():
    return [
        [8 * x + 2 * y + c for y in range(RING)] for x in range(RING) for c in range(CORES)
    ]


def ring_x(d):
    return [
        (8 * x + m, 8 * ((x + d) % RING) + m) for x in range(RING) for m in range(RING * CORES)
    ]


def ring_z(d):
    return [(z, (z + d) % RING) for z in range(RING)]


def other_core():
    return [(b, b ^ 1) for b in range(RING * RING * CORES)]


def over_y(pb):
    return [pb[0]] + [lax.ppermute(pb[d], "blk", ring_y(d)) for d in (1, 2, 3)]


def packed_form(
    slots,
    pb_y,
    pa,
    rank,
    part,
    amplitudes,
    integrals,
    occ_irrep,
    virt_irrep,
    occ_energy,
    virt_energy,
    slab_i,
    slab_j,
    slab_k,
):
    n_k, n_i, rows, wide = amplitudes.shape
    n_j = integrals.shape[1]
    kept = integrals.shape[3]
    half = LANES
    n_rest = pa.shape[2]
    groups = n_i // (n_rest - n_i)
    n_cols = RING * CORES * slots
    held = n_i * CORES * slots // LANES
    lv = virt_irrep.reshape(1, wide)
    ve = virt_energy.reshape(1, wide)
    row_spec = whole((1, wide))
    params = pltpu.CompilerParams(vmem_limit_bytes=32 * 1024 * 1024)

    pa_y = lax.all_to_all(pa, "blk", 0, 0, axis_index_groups=groups_y())

    m_rows = RING * n_i * rows
    spread = pl.pallas_call(
        unpack_kernel,
        grid=(n_k,),
        out_shape=jax.ShapeDtypeStruct((n_k, m_rows, wide), BF16),
        in_specs=[SMEM] * 3
        + [row_spec] * 2
        + [pl.BlockSpec((RING, 1, n_rest, rows, half), lambda k: (0, k, 0, 0, 0))],
        out_specs=pl.BlockSpec((1, m_rows, wide), lambda k: (k, 0, 0)),
        scratch_shapes=[
            pltpu.VMEM((groups, 2 * half, wide), BF16),
            pltpu.VMEM((1, wide), BF16),
            pltpu.VMEM((RING, rows, 1), I32),
        ],
        compiler_params=params,
        cost_estimate=cost(2 * n_k * m_rows * wide * 256, 20 << 20),
        name="unpack",
    )(occ_irrep, slab_i, slab_k, lv, rank, pa_y)

    mine = jnp.stack(pb_y)
    across = [mine] + [lax.ppermute(mine, "blk", ring_x(d)) for d in (1, 2, 3)]
    *across[2:], spread = lax.optimization_barrier((*across[2:], spread))
    twin = [lax.ppermute(b, "blk", other_core()) for b in across]
    parts = {}
    for first in (0, 2):
        parts[STEPS[first]], parts[STEPS[first + 1]] = pl.pallas_call(
            functools.partial(cycle_kernel, n_i, slots, first),
            grid=(n_k,),
            out_shape=[jax.ShapeDtypeStruct((RING, held, rows, LANES), F32)] * 2,
            in_specs=[pl.BlockSpec((1, m_rows, wide), lambda k: (k, 0, 0))]
            + [pl.BlockSpec((RING, 1, rows, n_cols), lambda k: (0, k, 0, 0))] * 8,
            out_specs=[whole((RING, held, rows, LANES))] * 2,
            scratch_shapes=[pltpu.VMEM((wide, 256), BF16), pltpu.VMEM((m_rows, 256), F32)],
            compiler_params=params,
            cost_estimate=cost(2 * n_k * m_rows * wide * 256, 14 << 20),
            name="cycle",
        )(spread, *across, *twin)

    sums = [parts[0]] + [lax.ppermute(parts[d], "red", ring_z(d)) for d in (1, 2, 3)]
    terms = pl.pallas_call(
        sum_kernel,
        grid=(2,),
        out_shape=[jax.ShapeDtypeStruct((held, rows, LANES), F32)] * RING,
        in_specs=[pl.BlockSpec((RING, held // 2, rows, LANES), lambda n: (0, n, 0, 0))] * RING,
        out_specs=[pl.BlockSpec((held // 2, rows, LANES), lambda n: (n, 0, 0))] * RING,
        compiler_params=params,
        cost_estimate=cost(m_rows * 512, 3 << 20),
        name="sums",
    )(*sums)
    back = [terms[0]] + [lax.ppermute(terms[d], "blk", ring_y(RING - d)) for d in (1, 2, 3)]

    return pl.pallas_call(
        functools.partial(update_kernel, slots),
        grid=(n_i // 2,),
        out_shape=jax.ShapeDtypeStruct(integrals.shape, F32),
        in_specs=[SMEM] * 4
        + [row_spec] * 3
        + [whole((held, rows, LANES))] * RING
        + [pl.BlockSpec((2, n_j, rows, kept), lambda n: (n, 0, 0, 0))],
        out_specs=pl.BlockSpec((2, n_j, rows, kept), lambda n: (n, 0, 0, 0)),
        scratch_shapes=[
            pltpu.VMEM((3 * LANES, CORES * kept), BF16),
            pltpu.VMEM((rows, 1), I32),
            pltpu.VMEM((rows, 1), F32),
            pltpu.VMEM((n_i, RING * rows, 3 * LANES), BF16),
        ],
        compiler_params=params,
        cost_estimate=cost(2 * 3 * m_rows * 128 * 512, 4 << 20),
        name="update",
    )(occ_irrep, slab_i, slab_j, occ_energy, lv, ve, part, *back, integrals)


def on_device(
    amplitudes,
    dressed,
    integrals,
    occ_irrep,
    virt_irrep,
    occ_energy,
    virt_energy,
    slab_i,
    slab_j,
    slab_k,
):
    pb_y, rank, part, fits = pack_dressed(
        PARTS[1], dressed, occ_irrep, virt_irrep, slab_j, slab_k
    )
    pb_y = over_y(pb_y)
    pa = pack_amplitudes(WIDES[1], amplitudes, rank, occ_irrep, virt_irrep, slab_i, slab_k)
    rest = (integrals, occ_irrep, virt_irrep, occ_energy, virt_energy, slab_i, slab_j, slab_k)

    def dense(pb_y, pa, rank, part, fits, a, d, *rest):
        return dense_form(a, d, *rest)

    def loose(pb_y, pa, rank, part, fits, a, d, *rest):
        pb, rank, part, _ = pack_dressed(PARTS[0], d, rest[1], rest[2], rest[6], rest[7])
        pa = pack_amplitudes(WIDES[0], a, rank, rest[1], rest[2], rest[5], rest[7])
        return packed_form(PARTS[0], over_y(pb), pa, rank, part, a, *rest)

    def tight(pb_y, pa, rank, part, fits, a, d, *rest):
        return packed_form(PARTS[1], pb_y, pa, rank, part, a, *rest)

    def other(pb_y, pa, rank, part, fits, *arrays):
        return lax.cond(fits[0] == 1, loose, dense, pb_y, pa, rank, part, fits, *arrays)

    return lax.cond(
        fits[0] == 2, tight, other, pb_y, pa, rank, part, fits, amplitudes, dressed, *rest
    )


def solution(mesh):
    in_specs = (
        P("red", None, "blk", None),
        P("red", None, "blk", None),
        P(None, None, "blk", "red"),
        P(),
        P(),
        P(),
        P(),
        P(),
        P(),
        P("red"),
    )
    out_specs = P(None, None, "blk", "red")
    return jax.shard_map(
        on_device, mesh=mesh, in_specs=in_specs, out_specs=out_specs, check_vma=False
    )
```

profile of v0, /device:TPU:0, one launch (start us, length us, event | category | flops | bytes accessed | tf_op | source)
XLA Modules:
  0.0 83.7 jit_solution(17921471072715266428)
XLA Ops:
  0.0 0.0 copy-start.2
  0.0 0.0 copy-start.3
  0.0 0.0 copy-start.5
  0.0 0.0 copy-start.4
  0.0 3.0 %pack_dressed.3 = (bf16[4,32,384]{2,1,0:T(8,128)(2,1)S(1)}, bf16[4,32,384]{2,1,0:T(8,128)(2,1)S(1)}, bf16[4,32,384]{2,1,0:T(8,128)(2,1)S(1)}, bf16[4,32,384]{2,1...) custom-call(s32[200]{0:T(256)} %occ_ref.3, s32[8]{0:T(128)} %sj_ref.1, s32[4]{0:T(128)} %sk_ref.3, ...), custom_call_target="tpu_custom_call" | custom-call | flops 536870912 | bytes 10485760 | tf_op jit(solution)/shard_map/pack_dressed/pallas_call | solution.py:473
  3.0 0.0 copy-start.6
  3.0 0.0 copy-start.7
  3.0 0.0 copy-start.8
  3.1 1.7 %collective-permute-start.29 = (bf16[4,32,384]{2,1,0:T(8,128)(2,1)S(1)}, bf16[4,32,384]{2,1,0:T(8,128)(2,1)S(1)}, u32[]{:S(2)}, u32[]{:S(2)}) collective-permute-start(bf16[4,32,384]{2,1,0:T(8,128)(2,1)S(1)} %get-tuple-element.198), channel_id=1, source_target_pairs={{0,8},{4,12},{8,16},{12,20},{16,24},{20,28},{24,0},{28,4},{32,40},... | collective-permute-start | bytes 294920 | tf_op jit(solution)/shard_map/ppermute | solution.py:546
  4.8 2.9 %collective-permute-start.30 = (bf16[4,32,384]{2,1,0:T(8,128)(2,1)S(1)}, bf16[4,32,384]{2,1,0:T(8,128)(2,1)}, u32[]{:S(2)}, u32[]{:S(2)}) collective-permute-start(bf16[4,32,384]{2,1,0:T(8,128)(2,1)S(1)} %get-tuple-element.199), channel_id=1, source_target_pairs={{0,16},{4,20},{8,24},{12,28},{16,0},{20,4},{24,8},{28,12},{32,48},... | collective-permute-start | bytes 294920 | tf_op jit(solution)/shard_map/ppermute | solution.py:546
  7.7 1.3 %collective-permute-start.31 = (bf16[4,32,384]{2,1,0:T(8,128)(2,1)S(1)}, bf16[4,32,384]{2,1,0:T(8,128)(2,1)}, u32[]{:S(2)}, u32[]{:S(2)}) collective-permute-start(bf16[4,32,384]{2,1,0:T(8,128)(2,1)S(1)} %get-tuple-element.200), channel_id=1, source_target_pairs={{0,24},{4,28},{8,0},{12,4},{16,8},{20,12},{24,16},{28,20},{32,56},... | collective-permute-start | bytes 294920 | tf_op jit(solution)/shard_map/ppermute | solution.py:546
  9.6 0.0 copy-done.2
  9.6 0.0 copy-done.3
  9.6 0.0 copy-done.5
  9.6 0.0 copy-done.4
  9.7 4.2 %pack_amplitudes.3 = bf16[4,4,10,32,128]{4,3,2,1,0:T(8,128)(2,1)} custom-call(s32[200]{0:T(256)S(1)} %copy-done.3, s32[8]{0:T(128)S(1)} %copy-done.4, s32[4]{0:T(128)S(1)} %copy-done.5, s32[1,1024]{1,0:T(1,128)S(1)} %bitcast.61, s32[1,1024]{1,0:T(1,128)S(1)} %get-tuple-element.201.rank_ref, bf16[4,8,32,1024]{3,2,1,0:T(8,128)(2,1)} %amp_ref.1), custom_call_target="tpu_custom_call" | custom-call | flops 536870912 | bytes 10485760 | tf_op jit(solution)/shard_map/pack_amplitudes/pallas_call | solution.py:498
  13.8 0.0 collective-permute-done.29
  13.8 0.0 collective-permute-done.30
  13.8 0.0 collective-permute-done.31
  13.8 0.0 copy-done.6
  13.8 0.0 copy-done.7
  13.9 0.0 copy-done.8
  13.9 69.9 %conditional.2 = (f32[8,8,32,256]{3,2,1,0:T(8,128)}) conditional(s32[]{:T(128)} %bitcast.32, (s32[1]{0:T(128)}, s32[8]{0:T(128)S(1)}, s32[200]{0:T(256)S(1)}, s32[8]{0:T(128)S(1)}, s32[1024]{0:T(1024)S(1)}, /*index=5*/bf16[8,8,32,256]{3,2,1,0:T(8,128)(2,1)}, (), s32[4]{0:T(128)S(1)}, bf16[4,8,32,1024]{3,2,1,0:T(8,128)(2,1)}, (), ...), branch_computations={%region_0.9_spmd, %region_9.10_spmd} | conditional | flops 17191471104 | bytes 320185760 | solution.py:685
  14.1 3.6 %all-to-all-start.1 = ((bf16[4,4,10,32,128]{4,3,2,1,0:T(8,128)(2,1)}), bf16[4,4,10,32,128]{4,3,2,1,0:T(8,128)(2,1)S(1)}, u32[]{:S(2)}, u32[]{:S(2)}) async-start(bf16[4,4,10,32,128]{4,3,2,1,0:T(8,128)(2,1)} %get-tuple-element.176), calls=%async_computation.1 | async-start | bytes 2621440 | tf_op jit(solution)/shard_map/cond/branch_1_fun/all_to_all | solution.py:578
  17.7 1.0 %pad_maximum_fusion.1.b0 = bf16[4,4,32,384]{3,2,1,0:T(8,128)(2,1)S(1)} fusion(bf16[1,4,32,384]{3,2,1,0:T(8,128)(2,1)} %bitcast.30, bf16[1,4,32,384]{3,2,1,0:T(8,128)(2,1)} %bitcast.29, bf16[1,4,32,384]{3,2,1,0:T(8,128)(2,1)S(1)} %bitcast.72, bf16[1,4,32,384]{3,2,1,0:T(8,128)(2,1)S(1)} %bitcast.71), kind=kLoop, calls=%fused_computation.3 | loop fusion | flops 589824 | bytes 786432 | tf_op jit(solution)/shard_map/cond/branch_1_fun/stack | solution.py:599
  18.7 1.6 %collective-permute-start.18 = (bf16[4,4,32,384]{3,2,1,0:T(8,128)(2,1)S(1)}, bf16[4,4,32,384]{3,2,1,0:T(8,128)(2,1)S(1)}, u32[]{:S(2)}, u32[]{:S(2)}) collective-permute-start(bf16[4,4,32,384]{3,2,1,0:T(8,128)(2,1)S(1)} %pad_maximum_fusion.1.b0), channel_id=1, source_target_pairs={{0,32},{4,36},{8,40},{12,44},{16,48},{20,52},{24,56},{28,60},{32,6... | collective-permute-start | bytes 1179656 | tf_op jit(solution)/shard_map/cond/branch_1_fun/ppermute | solution.py:600
  20.2 2.7 %collective-permute-start.16 = (bf16[4,4,32,384]{3,2,1,0:T(8,128)(2,1)S(1)}, bf16[4,4,32,384]{3,2,1,0:T(8,128)(2,1)S(1)}, u32[]{:S(2)}, u32[]{:S(2)}) collective-permute-start(bf16[4,4,32,384]{3,2,1,0:T(8,128)(2,1)S(1)} %pad_maximum_fusion.1.b0), channel_id=1, source_target_pairs={{0,64},{4,68},{8,72},{12,76},{16,80},{20,84},{24,88},{28,92},{32,9... | collective-permute-start | bytes 1179656 | tf_op jit(solution)/shard_map/cond/branch_1_fun/ppermute | solution.py:600
  23.0 1.4 %collective-permute-start.17 = (bf16[4,4,32,384]{3,2,1,0:T(8,128)(2,1)S(1)}, bf16[4,4,32,384]{3,2,1,0:T(8,128)(2,1)S(1)}, u32[]{:S(2)}, u32[]{:S(2)}) collective-permute-start(bf16[4,4,32,384]{3,2,1,0:T(8,128)(2,1)S(1)} %pad_maximum_fusion.1.b0), channel_id=1, source_target_pairs={{0,96},{4,100},{8,104},{12,108},{16,112},{20,116},{24,120},{28,124... | collective-permute-start | bytes 1179656 | tf_op jit(solution)/shard_map/cond/branch_1_fun/ppermute | solution.py:600
  24.4 0.0 collective-permute-start.19
  24.4 6.6 %collective-permute-done.18.b1 = bf16[4,4,32,384]{3,2,1,0:T(8,128)(2,1)S(1)} collective-permute-done((bf16[4,4,32,384]{3,2,1,0:T(8,128)(2,1)S(1)}, bf16[4,4,32,384]{3,2,1,0:T(8,128)(2,1)S(1)}, u32[]{:S(2)}, u32[]{:S(2)}) %collective-permute-start.18) | collective-permute-done | bytes 393248 | tf_op jit(solution)/shard_map/cond/branch_1_fun/ppermute | solution.py:600
  31.0 0.0 collective-permute-start.20
  31.0 4.0 %all-to-all-done.1.pa_ref = bf16[4,4,10,32,128]{4,3,2,1,0:T(8,128)(2,1)S(1)} async-done(((bf16[4,4,10,32,128]{4,3,2,1,0:T(8,128)(2,1)}), bf16[4,4,10,32,128]{4,3,2,1,0:T(8,128)(2,1)S(1)}, u32[]{:S(2)}, u32[]{:S(2)}) %all-to-all-start.1) | async-done | bytes 1310752 | tf_op jit(solution)/shard_map/cond/branch_1_fun/all_to_all | solution.py:578
  35.0 4.6 %unpack.3.a_ref = bf16[4,1024,1024]{2,1,0:T(8,128)(2,1)S(1)} custom-call(s32[200]{0:T(256)S(1)} %get-tuple-element.163.occ_ref, s32[8]{0:T(128)S(1)} %get-tuple-element.164.si_ref, s32[4]{0:T(128)S(1)} %get-tuple-element.174.sk_ref, s32[1,1024]{1,0:T(1,128)S(1)} %bitcast.66, s32[1,1024]{1,0:T(1,128)S(1)} %get-tuple-element.175.rank_ref, ...), custom_call_target="tpu_custom_call" | custom-call | flops 2147483648 | bytes 20971520 | tf_op jit(solution)/shard_map/cond/branch_1_fun/unpack/pallas_call | solution.py:581
  39.6 0.0 collective-permute-done.16.b2
  39.6 0.0 collective-permute-done.17.b3
  39.6 0.1 collective-permute-start.21
  39.7 0.5 collective-permute-start.22
  40.2 0.0 collective-permute-done.19.b4
  40.2 0.0 collective-permute-done.20.b5
  40.2 1.2 %collective-permute-done.21.b6 = bf16[4,4,32,384]{3,2,1,0:T(8,128)(2,1)S(1)} collective-permute-done((bf16[4,4,32,384]{3,2,1,0:T(8,128)(2,1)S(1)}, bf16[4,4,32,384]{3,2,1,0:T(8,128)(2,1)S(1)}, u32[]{:S(2)}, u32[]{:S(2)}) %collective-permute-start.21) | collective-permute-done | bytes 393248 | tf_op jit(solution)/shard_map/cond/branch_1_fun/ppermute | solution.py:602
  41.4 0.6 collective-permute-done.22.b7
  41.9 4.8 %cycle.7 = (f32[4,6,32,128]{3,2,1,0:T(8,128)S(1)}, f32[4,6,32,128]{3,2,1,0:T(8,128)S(1)}) custom-call(bf16[4,1024,1024]{2,1,0:T(8,128)(2,1)S(1)} %unpack.3.a_ref, bf16[4,4,32,384]{3,2,1,0:T(8,128)(2,1)S(1)} %pad_maximum_fusion.1.b0, bf16[4,4,32,384]{3,2,1,0:T(8,128)(2,1)S(1)} %collective-permute-done.18.b1, ...), custom_call_target="tpu_custom_call" | custom-call | flops 2147483648 | bytes 14680064 | tf_op jit(solution)/shard_map/cond/branch_1_fun/cycle/pallas_call | solution.py:605
  46.7 2.0 %collective-permute-start.23 = (f32[4,6,32,128]{3,2,1,0:T(8,128)S(1)}, f32[4,6,32,128]{3,2,1,0:T(8,128)S(1)}, u32[]{:S(2)}, u32[]{:S(2)}) collective-permute-start(f32[4,6,32,128]{3,2,1,0:T(8,128)S(1)} %get-tuple-element.181), channel_id=1, source_target_pairs={{0,1},{1,2},{2,3},{3,0},{4,5},{5,6},{6,7},{7,4},{8,9},{9,10},{10,1... | collective-permute-start | bytes 1179656 | tf_op jit(solution)/shard_map/cond/branch_1_fun/ppermute | solution.py:618
  48.7 2.2 %collective-permute-start.25 = (f32[4,6,32,128]{3,2,1,0:T(8,128)S(1)}, f32[4,6,32,128]{3,2,1,0:T(8,128)S(1)}, u32[]{:S(2)}, u32[]{:S(2)}) collective-permute-start(f32[4,6,32,128]{3,2,1,0:T(8,128)S(1)} %get-tuple-element.183), channel_id=1, source_target_pairs={{0,3},{1,0},{2,1},{3,2},{4,7},{5,4},{6,5},{7,6},{8,11},{9,8},{10,9... | collective-permute-start | bytes 1179656 | tf_op jit(solution)/shard_map/cond/branch_1_fun/ppermute | solution.py:618
  50.9 4.9 %cycle.6 = (f32[4,6,32,128]{3,2,1,0:T(8,128)S(1)}, f32[4,6,32,128]{3,2,1,0:T(8,128)S(1)}) custom-call(bf16[4,1024,1024]{2,1,0:T(8,128)(2,1)S(1)} %unpack.3.a_ref, bf16[4,4,32,384]{3,2,1,0:T(8,128)(2,1)S(1)} %pad_maximum_fusion.1.b0, bf16[4,4,32,384]{3,2,1,0:T(8,128)(2,1)S(1)} %collective-permute-done.18.b1, ...), custom_call_target="tpu_custom_call" | custom-call | flops 2147483648 | bytes 14680064 | tf_op jit(solution)/shard_map/cond/branch_1_fun/cycle/pallas_call | solution.py:605
  55.8 0.0 copy-start.1
  55.8 1.9 %collective-permute-start.24 = (f32[4,6,32,128]{3,2,1,0:T(8,128)S(1)}, f32[4,6,32,128]{3,2,1,0:T(8,128)S(1)}, u32[]{:S(2)}, u32[]{:S(2)}) collective-permute-start(f32[4,6,32,128]{3,2,1,0:T(8,128)S(1)} %get-tuple-element.182), channel_id=1, source_target_pairs={{0,2},{1,3},{2,0},{3,1},{4,6},{5,7},{6,4},{7,5},{8,10},{9,11},{10,... | collective-permute-start | bytes 1179656 | tf_op jit(solution)/shard_map/cond/branch_1_fun/ppermute | solution.py:618
  57.7 2.6 %collective-permute-done.23.o1 = f32[4,6,32,128]{3,2,1,0:T(8,128)S(1)} collective-permute-done((f32[4,6,32,128]{3,2,1,0:T(8,128)S(1)}, f32[4,6,32,128]{3,2,1,0:T(8,128)S(1)}, u32[]{:S(2)}, u32[]{:S(2)}) %collective-permute-start.23) | collective-permute-done | bytes 393248 | tf_op jit(solution)/shard_map/cond/branch_1_fun/ppermute | solution.py:618
  60.3 7.8 %collective-permute-done.25.o3 = f32[4,6,32,128]{3,2,1,0:T(8,128)S(1)} collective-permute-done((f32[4,6,32,128]{3,2,1,0:T(8,128)S(1)}, f32[4,6,32,128]{3,2,1,0:T(8,128)S(1)}, u32[]{:S(2)}, u32[]{:S(2)}) %collective-permute-start.25) | collective-permute-done | bytes 393248 | tf_op jit(solution)/shard_map/cond/branch_1_fun/ppermute | solution.py:618
  68.1 1.8 %collective-permute-done.24.o2 = f32[4,6,32,128]{3,2,1,0:T(8,128)S(1)} collective-permute-done((f32[4,6,32,128]{3,2,1,0:T(8,128)S(1)}, f32[4,6,32,128]{3,2,1,0:T(8,128)S(1)}, u32[]{:S(2)}, u32[]{:S(2)}) %collective-permute-start.24) | collective-permute-done | bytes 393248 | tf_op jit(solution)/shard_map/cond/branch_1_fun/ppermute | solution.py:618
  69.9 0.2 sums.3
  70.1 2.7 %collective-permute-start.26 = (f32[6,32,128]{2,1,0:T(8,128)S(1)}, f32[6,32,128]{2,1,0:T(8,128)S(1)}, u32[]{:S(2)}, u32[]{:S(2)}) collective-permute-start(f32[6,32,128]{2,1,0:T(8,128)S(1)} %get-tuple-element.185), channel_id=1, source_target_pairs={{0,24},{4,28},{8,0},{12,4},{16,8},{20,12},{24,16},{28,20},{32,56},... | collective-permute-start | bytes 294920 | tf_op jit(solution)/shard_map/cond/branch_1_fun/ppermute | solution.py:629
  72.8 0.9 %collective-permute-start.27 = (f32[6,32,128]{2,1,0:T(8,128)S(1)}, f32[6,32,128]{2,1,0:T(8,128)S(1)}, u32[]{:S(2)}, u32[]{:S(2)}) collective-permute-start(f32[6,32,128]{2,1,0:T(8,128)S(1)} %get-tuple-element.186), channel_id=1, source_target_pairs={{0,16},{4,20},{8,24},{12,28},{16,0},{20,4},{24,8},{28,12},{32,48},... | collective-permute-start | bytes 294920 | tf_op jit(solution)/shard_map/cond/branch_1_fun/ppermute | solution.py:629
  73.7 0.9 %collective-permute-start.28 = (f32[6,32,128]{2,1,0:T(8,128)S(1)}, f32[6,32,128]{2,1,0:T(8,128)S(1)}, u32[]{:S(2)}, u32[]{:S(2)}) collective-permute-start(f32[6,32,128]{2,1,0:T(8,128)S(1)} %get-tuple-element.187), channel_id=1, source_target_pairs={{0,8},{4,12},{8,16},{12,20},{16,24},{20,28},{24,0},{28,4},{32,40},... | collective-permute-start | bytes 294920 | tf_op jit(solution)/shard_map/cond/branch_1_fun/ppermute | solution.py:629
  74.5 2.1 %collective-permute-done.26.t1 = f32[6,32,128]{2,1,0:T(8,128)S(1)} collective-permute-done((f32[6,32,128]{2,1,0:T(8,128)S(1)}, f32[6,32,128]{2,1,0:T(8,128)S(1)}, u32[]{:S(2)}, u32[]{:S(2)}) %collective-permute-start.26) | collective-permute-done | bytes 98336 | tf_op jit(solution)/shard_map/cond/branch_1_fun/ppermute | solution.py:629
  76.7 2.5 %collective-permute-done.27.t2 = f32[6,32,128]{2,1,0:T(8,128)S(1)} collective-permute-done((f32[6,32,128]{2,1,0:T(8,128)S(1)}, f32[6,32,128]{2,1,0:T(8,128)S(1)}, u32[]{:S(2)}, u32[]{:S(2)}) %collective-permute-start.27) | collective-permute-done | bytes 98336 | tf_op jit(solution)/shard_map/cond/branch_1_fun/ppermute | solution.py:629
  79.2 1.0 %collective-permute-done.28.t3 = f32[6,32,128]{2,1,0:T(8,128)S(1)} collective-permute-done((f32[6,32,128]{2,1,0:T(8,128)S(1)}, f32[6,32,128]{2,1,0:T(8,128)S(1)}, u32[]{:S(2)}, u32[]{:S(2)}) %collective-permute-start.28) | collective-permute-done | bytes 98336 | tf_op jit(solution)/shard_map/cond/branch_1_fun/ppermute | solution.py:629
  80.2 0.0 copy-done.1
  80.2 3.6 %update.3 = f32[8,8,32,256]{3,2,1,0:T(8,128)} custom-call(s32[200]{0:T(256)S(1)} %get-tuple-element.163.occ_ref, s32[8]{0:T(128)S(1)} %get-tuple-element.164.si_ref, s32[8]{0:T(128)S(1)} %get-tuple-element.165.sj_ref, f32[200]{0:T(256)S(1)} %get-tuple-element.166.oe_ref, s32[1,1024]{1,0:T(1,128)S(1)} %bitcast.67, f32[1,1024]{1,0:T(1,128)S(1)} %bitcast.74, ...), custom_call_target="tpu_custom_call" | custom-call | flops 402653184 | bytes 4194304 | tf_op jit(solution)/shard_map/cond/branch_1_fun/update/pallas_call | solution.py:631
Async XLA Ops:
  0.0 9.6 %copy-start.2 = (s32[1024]{0:T(1024)S(1)}, s32[1024]{0:T(1024)}, u32[]{:S(2)}) copy-start(s32[1024]{0:T(1024)} %param.20) | copy-start | bytes 12292
  0.0 9.6 %copy-start.3 = (s32[200]{0:T(256)S(1)}, s32[200]{0:T(256)}, u32[]{:S(2)}) copy-start(s32[200]{0:T(256)} %occ_ref.3) | copy-start | bytes 2404
  0.0 9.6 %copy-start.5 = (s32[4]{0:T(128)S(1)}, s32[4]{0:T(128)}, u32[]{:S(2)}) copy-start(s32[4]{0:T(128)} %sk_ref.3) | copy-start | bytes 52
  0.0 9.6 %copy-start.4 = (s32[8]{0:T(128)S(1)}, s32[8]{0:T(128)}, u32[]{:S(2)}) copy-start(s32[8]{0:T(128)} %si_ref.1) | copy-start | bytes 100
  3.0 10.8 %copy-start.6 = (f32[1024]{0:T(1024)S(1)}, f32[1024]{0:T(1024)}, u32[]{:S(2)}) copy-start(f32[1024]{0:T(1024)} %param.22) | copy-start | bytes 12292
  3.0 10.8 %copy-start.7 = (s32[8]{0:T(128)S(1)}, s32[8]{0:T(128)}, u32[]{:S(2)}) copy-start(s32[8]{0:T(128)} %sj_ref.1) | copy-start | bytes 100
  3.0 10.8 %copy-start.8 = (f32[200]{0:T(256)S(1)}, f32[200]{0:T(256)}, u32[]{:S(2)}) copy-start(f32[200]{0:T(256)} %param.21) | copy-start | bytes 2404
  3.1 10.8 %collective-permute-start.29 = (bf16[4,32,384]{2,1,0:T(8,128)(2,1)S(1)}, bf16[4,32,384]{2,1,0:T(8,128)(2,1)S(1)}, u32[]{:S(2)}, u32[]{:S(2)}) collective-permute-start(bf16[4,32,384]{2,1,0:T(8,128)(2,1)S(1)} %get-tuple-element.198), channel_id=1, source_target_pairs={{0,8},{4,12},{8,16},{12,20},{16,24},{20,28},{24,0},{28,4},{32,40},... | collective-permute-start | bytes 294920 | tf_op jit(solution)/shard_map/ppermute | solution.py:546
  4.8 9.0 %collective-permute-start.30 = (bf16[4,32,384]{2,1,0:T(8,128)(2,1)S(1)}, bf16[4,32,384]{2,1,0:T(8,128)(2,1)}, u32[]{:S(2)}, u32[]{:S(2)}) collective-permute-start(bf16[4,32,384]{2,1,0:T(8,128)(2,1)S(1)} %get-tuple-element.199), channel_id=1, source_target_pairs={{0,16},{4,20},{8,24},{12,28},{16,0},{20,4},{24,8},{28,12},{32,48},... | collective-permute-start | bytes 294920 | tf_op jit(solution)/shard_map/ppermute | solution.py:546
  7.7 6.1 %collective-permute-start.31 = (bf16[4,32,384]{2,1,0:T(8,128)(2,1)S(1)}, bf16[4,32,384]{2,1,0:T(8,128)(2,1)}, u32[]{:S(2)}, u32[]{:S(2)}) collective-permute-start(bf16[4,32,384]{2,1,0:T(8,128)(2,1)S(1)} %get-tuple-element.200), channel_id=1, source_target_pairs={{0,24},{4,28},{8,0},{12,4},{16,8},{20,12},{24,16},{28,20},{32,56},... | collective-permute-start | bytes 294920 | tf_op jit(solution)/shard_map/ppermute | solution.py:546
  14.1 20.9 %all-to-all-start.1 = ((bf16[4,4,10,32,128]{4,3,2,1,0:T(8,128)(2,1)}), bf16[4,4,10,32,128]{4,3,2,1,0:T(8,128)(2,1)S(1)}, u32[]{:S(2)}, u32[]{:S(2)}) async-start(bf16[4,4,10,32,128]{4,3,2,1,0:T(8,128)(2,1)} %get-tuple-element.176), calls=%async_computation.1 | async-start | bytes 2621440 | tf_op jit(solution)/shard_map/cond/branch_1_fun/all_to_all | solution.py:578
  18.7 12.3 %collective-permute-start.18 = (bf16[4,4,32,384]{3,2,1,0:T(8,128)(2,1)S(1)}, bf16[4,4,32,384]{3,2,1,0:T(8,128)(2,1)S(1)}, u32[]{:S(2)}, u32[]{:S(2)}) collective-permute-start(bf16[4,4,32,384]{3,2,1,0:T(8,128)(2,1)S(1)} %pad_maximum_fusion.1.b0), channel_id=1, source_target_pairs={{0,32},{4,36},{8,40},{12,44},{16,48},{20,52},{24,56},{28,60},{32,6... | collective-permute-start | bytes 1179656 | tf_op jit(solution)/shard_map/cond/branch_1_fun/ppermute | solution.py:600
  20.2 19.3 %collective-permute-start.16 = (bf16[4,4,32,384]{3,2,1,0:T(8,128)(2,1)S(1)}, bf16[4,4,32,384]{3,2,1,0:T(8,128)(2,1)S(1)}, u32[]{:S(2)}, u32[]{:S(2)}) collective-permute-start(bf16[4,4,32,384]{3,2,1,0:T(8,128)(2,1)S(1)} %pad_maximum_fusion.1.b0), channel_id=1, source_target_pairs={{0,64},{4,68},{8,72},{12,76},{16,80},{20,84},{24,88},{28,92},{32,9... | collective-permute-start | bytes 1179656 | tf_op jit(solution)/shard_map/cond/branch_1_fun/ppermute | solution.py:600
  23.0 16.6 %collective-permute-start.17 = (bf16[4,4,32,384]{3,2,1,0:T(8,128)(2,1)S(1)}, bf16[4,4,32,384]{3,2,1,0:T(8,128)(2,1)S(1)}, u32[]{:S(2)}, u32[]{:S(2)}) collective-permute-start(bf16[4,4,32,384]{3,2,1,0:T(8,128)(2,1)S(1)} %pad_maximum_fusion.1.b0), channel_id=1, source_target_pairs={{0,96},{4,100},{8,104},{12,108},{16,112},{20,116},{24,120},{28,124... | collective-permute-start | bytes 1179656 | tf_op jit(solution)/shard_map/cond/branch_1_fun/ppermute | solution.py:600
  24.4 15.8 %collective-permute-start.19 = (bf16[4,4,32,384]{3,2,1,0:T(8,128)(2,1)S(1)}, bf16[4,4,32,384]{3,2,1,0:T(8,128)(2,1)S(1)}, u32[]{:S(2)}, u32[]{:S(2)}) collective-permute-start(bf16[4,4,32,384]{3,2,1,0:T(8,128)(2,1)S(1)} %pad_maximum_fusion.1.b0), channel_id=1, source_target_pairs={{0,4},{4,0},{8,12},{12,8},{16,20},{20,16},{24,28},{28,24},{32,36},... | collective-permute-start | bytes 1179656 | tf_op jit(solution)/shard_map/cond/branch_1_fun/ppermute | solution.py:602
  31.0 9.2 %collective-permute-start.20 = (bf16[4,4,32,384]{3,2,1,0:T(8,128)(2,1)S(1)}, bf16[4,4,32,384]{3,2,1,0:T(8,128)(2,1)}, u32[]{:S(2)}, u32[]{:S(2)}) collective-permute-start(bf16[4,4,32,384]{3,2,1,0:T(8,128)(2,1)S(1)} %collective-permute-done.18.b1), channel_id=1, source_target_pairs={{0,4},{4,0},{8,12},{12,8},{16,20},{20,16},{24,28},{28,24},{32,36},... | collective-permute-start | bytes 1179656 | tf_op jit(solution)/shard_map/cond/branch_1_fun/ppermute | solution.py:602
  39.6 1.8 %collective-permute-start.21 = (bf16[4,4,32,384]{3,2,1,0:T(8,128)(2,1)S(1)}, bf16[4,4,32,384]{3,2,1,0:T(8,128)(2,1)S(1)}, u32[]{:S(2)}, u32[]{:S(2)}) collective-permute-start(bf16[4,4,32,384]{3,2,1,0:T(8,128)(2,1)S(1)} %collective-permute-done.16.b2), channel_id=1, source_target_pairs={{0,4},{4,0},{8,12},{12,8},{16,20},{20,16},{24,28},{28,24},{32,36},... | collective-permute-start | bytes 1179656 | tf_op jit(solution)/shard_map/cond/branch_1_fun/ppermute | solution.py:602
  39.7 2.3 %collective-permute-start.22 = (bf16[4,4,32,384]{3,2,1,0:T(8,128)(2,1)S(1)}, bf16[4,4,32,384]{3,2,1,0:T(8,128)(2,1)S(1)}, u32[]{:S(2)}, u32[]{:S(2)}) collective-permute-start(bf16[4,4,32,384]{3,2,1,0:T(8,128)(2,1)S(1)} %collective-permute-done.17.b3), channel_id=1, source_target_pairs={{0,4},{4,0},{8,12},{12,8},{16,20},{20,16},{24,28},{28,24},{32,36},... | collective-permute-start | bytes 1179656 | tf_op jit(solution)/shard_map/cond/branch_1_fun/ppermute | solution.py:602
  46.7 13.5 %collective-permute-start.23 = (f32[4,6,32,128]{3,2,1,0:T(8,128)S(1)}, f32[4,6,32,128]{3,2,1,0:T(8,128)S(1)}, u32[]{:S(2)}, u32[]{:S(2)}) collective-permute-start(f32[4,6,32,128]{3,2,1,0:T(8,128)S(1)} %get-tuple-element.181), channel_id=1, source_target_pairs={{0,1},{1,2},{2,3},{3,0},{4,5},{5,6},{6,7},{7,4},{8,9},{9,10},{10,1... | collective-permute-start | bytes 1179656 | tf_op jit(solution)/shard_map/cond/branch_1_fun/ppermute | solution.py:618
  48.7 19.3 %collective-permute-start.25 = (f32[4,6,32,128]{3,2,1,0:T(8,128)S(1)}, f32[4,6,32,128]{3,2,1,0:T(8,128)S(1)}, u32[]{:S(2)}, u32[]{:S(2)}) collective-permute-start(f32[4,6,32,128]{3,2,1,0:T(8,128)S(1)} %get-tuple-element.183), channel_id=1, source_target_pairs={{0,3},{1,0},{2,1},{3,2},{4,7},{5,4},{6,5},{7,6},{8,11},{9,8},{10,9... | collective-permute-start | bytes 1179656 | tf_op jit(solution)/shard_map/cond/branch_1_fun/ppermute | solution.py:618
  55.8 24.4 %copy-start.1 = (bf16[8,8,32,256]{3,2,1,0:T(8,128)(2,1)S(1)}, bf16[8,8,32,256]{3,2,1,0:T(8,128)(2,1)}, u32[]{:S(2)}) copy-start(bf16[8,8,32,256]{3,2,1,0:T(8,128)(2,1)} %get-tuple-element.188.int_ref) | copy-start | bytes 3145732 | tf_op jit(solution)/shard_map/cond
  55.8 14.1 %collective-permute-start.24 = (f32[4,6,32,128]{3,2,1,0:T(8,128)S(1)}, f32[4,6,32,128]{3,2,1,0:T(8,128)S(1)}, u32[]{:S(2)}, u32[]{:S(2)}) collective-permute-start(f32[4,6,32,128]{3,2,1,0:T(8,128)S(1)} %get-tuple-element.182), channel_id=1, source_target_pairs={{0,2},{1,3},{2,0},{3,1},{4,6},{5,7},{6,4},{7,5},{8,10},{9,11},{10,... | collective-permute-start | bytes 1179656 | tf_op jit(solution)/shard_map/cond/branch_1_fun/ppermute | solution.py:618
  70.1 6.6 %collective-permute-start.26 = (f32[6,32,128]{2,1,0:T(8,128)S(1)}, f32[6,32,128]{2,1,0:T(8,128)S(1)}, u32[]{:S(2)}, u32[]{:S(2)}) collective-permute-start(f32[6,32,128]{2,1,0:T(8,128)S(1)} %get-tuple-element.185), channel_id=1, source_target_pairs={{0,24},{4,28},{8,0},{12,4},{16,8},{20,12},{24,16},{28,20},{32,56},... | collective-permute-start | bytes 294920 | tf_op jit(solution)/shard_map/cond/branch_1_fun/ppermute | solution.py:629
  72.8 6.3 %collective-permute-start.27 = (f32[6,32,128]{2,1,0:T(8,128)S(1)}, f32[6,32,128]{2,1,0:T(8,128)S(1)}, u32[]{:S(2)}, u32[]{:S(2)}) collective-permute-start(f32[6,32,128]{2,1,0:T(8,128)S(1)} %get-tuple-element.186), channel_id=1, source_target_pairs={{0,16},{4,20},{8,24},{12,28},{16,0},{20,4},{24,8},{28,12},{32,48},... | collective-permute-start | bytes 294920 | tf_op jit(solution)/shard_map/cond/branch_1_fun/ppermute | solution.py:629
  73.7 6.5 %collective-permute-start.28 = (f32[6,32,128]{2,1,0:T(8,128)S(1)}, f32[6,32,128]{2,1,0:T(8,128)S(1)}, u32[]{:S(2)}, u32[]{:S(2)}) collective-permute-start(f32[6,32,128]{2,1,0:T(8,128)S(1)} %get-tuple-element.187), channel_id=1, source_target_pairs={{0,8},{4,12},{8,16},{12,20},{16,24},{20,28},{24,0},{28,4},{32,40},... | collective-permute-start | bytes 294920 | tf_op jit(solution)/shard_map/cond/branch_1_fun/ppermute | solution.py:629
where the time goes:
time: 84.2 us; the launch traced here: 83.7 us
  waiting for transfers between devices  30.2 us (36%)
  starting transfers between devices  26.3 us (31%)
  Pallas kernels  25.2 us (30%)
  other arithmetic  1 us (1%)
    ppermute x3, waiting for transfers between devices, packed_form(): lax.ppermute(parts[d], 'red', ring_z(d))  12.2 us
    pallas_call x2, Pallas kernels, packed_form(): pl.pallas_call(functools.partial(cycle_kernel, n_i, slots, first), grid=(...  9.64 us
    ppermute x3, waiting for transfers between devices, packed_form(): across = [mine] + [lax.ppermute(mine, 'blk', ring_x(d)) for d in (1, 2, 3)]  6.62 us
    ppermute x3, starting transfers between devices, packed_form(): lax.ppermute(parts[d], 'red', ring_z(d))  6.05 us
    ppermute x3, starting transfers between devices, over_y(): return [pb[0]] + [lax.ppermute(pb[d], 'blk', ring_y(d)) for d in (1, 2, 3)]  5.99 us
    ppermute x3, starting transfers between devices, packed_form(): across = [mine] + [lax.ppermute(mine, 'blk', ring_x(d)) for d in (1, 2, 3)]  5.72 us
    ppermute x3, waiting for transfers between devices, packed_form(): lax.ppermute(terms[d], 'blk', ring_y(RING - d))  5.62 us
    pallas_call x1, Pallas kernels, packed_form(): pl.pallas_call(unpack_kernel, grid=(n_k,), out_shape=jax.ShapeDtypeStruct...  4.57 us
  transfers between devices with their start and end apart: 17, of which 10 were waited for; matrix products, arithmetic and copies ran while one was open for 1% of the time, Pallas kernels for 16%

commit v1 on v0

--- a/solution.py
+++ b/solution.py
@@ -294,30 +294,31 @@
             first = x * (rows * 8) + ((y - d + RING) % RING) * (rows * 2) + core * rows
             labels[d] = picked_column(lv_ref[...], first, rows)
 
-    lk = occ_ref[sk_ref[k]]
-    group = n_i // groups
-    blocks = [pa_ref.at[(y - d + RING) % RING] for d in range(RING)]
-    for side in range(groups):
-        pairs = []
-        for block in blocks:
-            main = block[0, side * group : (side + 1) * group].reshape(group * rows, half)
-            rest = block[0, n_i:].reshape(group * rows, half)
-            pairs.append(jnp.concatenate([main, rest], axis=1))
-        spread = jnp.dot(
-            jnp.concatenate(pairs, axis=0), hot[side], preferred_element_type=F32
-        )
-        for d in range(RING):
-            for g in range(group):
-                i = side * group + g
-                label = jnp.bitwise_xor(lk, occ_ref[si_ref[i]])
-                wanted = jnp.bitwise_xor(labels[d], label).astype(F32).astype(BF16)
-                at = (d * n_i + i) * rows
-                source = (d * group + g) * rows
-                out_ref[0, at : at + rows, :] = jnp.where(
-                    wanted == order[...],
-                    spread[source : source + rows].astype(BF16),
-                    jnp.zeros((), BF16),
-                )
+    for e in range(out_ref.shape[0]):
+        lk = occ_ref[sk_ref[k * out_ref.shape[0] + e]]
+        group = n_i // groups
+        blocks = [pa_ref.at[(y - d + RING) % RING] for d in range(RING)]
+        for side in range(groups):
+            pairs = []
+            for block in blocks:
+                main = block[e, side * group : (side + 1) * group].reshape(group * rows, half)
+                rest = block[e, n_i:].reshape(group * rows, half)
+                pairs.append(jnp.concatenate([main, rest], axis=1))
+            spread = jnp.dot(
+                jnp.concatenate(pairs, axis=0), hot[side], preferred_element_type=F32
+            )
+            for d in range(RING):
+                for g in range(group):
+                    i = side * group + g
+                    label = jnp.bitwise_xor(lk, occ_ref[si_ref[i]])
+                    wanted = jnp.bitwise_xor(labels[d], label).astype(F32).astype(BF16)
+                    at = (d * n_i + i) * rows
+                    source = (d * group + g) * rows
+                    out_ref[e, at : at + rows, :] = jnp.where(
+                        wanted == order[...],
+                        spread[source : source + rows].astype(BF16),
+                        jnp.zeros((), BF16),
+                    )
 
 
 def folded(value, n_i, rows):
@@ -345,9 +346,13 @@
     rows = b0.shape[2]
     depth = b0.shape[0] * rows
     start = first * CORES * slots // LANES * LANES
-    for n, b in enumerate((b0, b1, b2, b3, b4, b5, b6, b7)):
-        b_all[n * depth : (n + 1) * depth, :] = b[:, 0, :, start : start + 256].reshape(depth, 256)
-    term = jnp.dot(a_ref[0], b_all[...], preferred_element_type=F32)
+    term = None
+    for e in range(a_ref.shape[0]):
+        for n, b in enumerate((b0, b1, b2, b3, b4, b5, b6, b7)):
+            block = b[:, e, :, start : start + 256].reshape(depth, 256)
+            b_all[e, n * depth : (n + 1) * depth, :] = block
+        part = jnp.dot(a_ref[e], b_all[e], preferred_element_type=F32)
+        term = part if term is None else term + part
 
     @pl.when(k == 0)
     def _():
@@ -580,12 +585,12 @@
     m_rows = RING * n_i * rows
     spread = pl.pallas_call(
         unpack_kernel,
-        grid=(n_k,),
+        grid=(n_k // 2,),
         out_shape=jax.ShapeDtypeStruct((n_k, m_rows, wide), BF16),
         in_specs=[SMEM] * 3
         + [row_spec] * 2
-        + [pl.BlockSpec((RING, 1, n_rest, rows, half), lambda k: (0, k, 0, 0, 0))],
-        out_specs=pl.BlockSpec((1, m_rows, wide), lambda k: (k, 0, 0)),
+        + [pl.BlockSpec((RING, 2, n_rest, rows, half), lambda k: (0, k, 0, 0, 0))],
+        out_specs=pl.BlockSpec((2, m_rows, wide), lambda k: (k, 0, 0)),
         scratch_shapes=[
             pltpu.VMEM((groups, 2 * half, wide), BF16),
             pltpu.VMEM((1, wide), BF16),
@@ -604,12 +609,12 @@
     for first in (0, 2):
         parts[STEPS[first]], parts[STEPS[first + 1]] = pl.pallas_call(
             functools.partial(cycle_kernel, n_i, slots, first),
-            grid=(n_k,),
+            grid=(n_k // 2,),
             out_shape=[jax.ShapeDtypeStruct((RING, held, rows, LANES), F32)] * 2,
-            in_specs=[pl.BlockSpec((1, m_rows, wide), lambda k: (k, 0, 0))]
-            + [pl.BlockSpec((RING, 1, rows, n_cols), lambda k: (0, k, 0, 0))] * 8,
+            in_specs=[pl.BlockSpec((2, m_rows, wide), lambda k: (k, 0, 0))]
+            + [pl.BlockSpec((RING, 2, rows, n_cols), lambda k: (0, k, 0, 0))] * 8,
             out_specs=[whole((RING, held, rows, LANES))] * 2,
-            scratch_shapes=[pltpu.VMEM((wide, 256), BF16), pltpu.VMEM((m_rows, 256), F32)],
+            scratch_shapes=[pltpu.VMEM((2, wide, 256), BF16), pltpu.VMEM((m_rows, 256), F32)],
             compiler_params=params,
             cost_estimate=cost(2 * n_k * m_rows * wide * 256, 14 << 20),
             name="cycle",
@@ -630,13 +635,13 @@
 
     return pl.pallas_call(
         functools.partial(update_kernel, slots),
-        grid=(n_i // 2,),
+        grid=(n_i // 4,),
         out_shape=jax.ShapeDtypeStruct(integrals.shape, F32),
         in_specs=[SMEM] * 4
         + [row_spec] * 3
         + [whole((held, rows, LANES))] * RING
-        + [pl.BlockSpec((2, n_j, rows, kept), lambda n: (n, 0, 0, 0))],
-        out_specs=pl.BlockSpec((2, n_j, rows, kept), lambda n: (n, 0, 0, 0)),
+        + [pl.BlockSpec((4, n_j, rows, kept), lambda n: (n, 0, 0, 0))],
+        out_specs=pl.BlockSpec((4, n_j, rows, kept), lambda n: (n, 0, 0, 0)),
         scratch_shapes=[
             pltpu.VMEM((3 * LANES, CORES * kept), BF16),
             pltpu.VMEM((rows, 1), I32),

time: 84.2 us -> 82.7 us (0.982)
  Pallas kernels: 25.2 us -> 22.7 us
  waiting for transfers between devices: 30.2 us -> 31.2 us
    pallas_call x2, Pallas kernels: 9.64 us -> 8.24 us  [packed_form(): pl.pallas_call(functools.partial(cycle_kernel, n_i, slots, first), grid=(...]
    pallas_call x2, Pallas kernels: 8.14 us -> 7.03 us  [the longest x1 4.1 us: packed_form(): pl.pallas_call(unpack_kernel, grid=(n_k // 2,), out_shape=jax.ShapeDtypeS...]
  transfers between devices with their start and end apart: 17 -> 17, of which waited for: 10 -> 11; matrix products, arithmetic and copies ran while one was open for 1% -> 1% of each run, Pallas kernels for 16% -> 15%
where the time goes in v1:
time: 82.7 us; the launch traced here: 82.4 us
  waiting for transfers between devices  31.2 us (38%)
  starting transfers between devices  26.5 us (32%)
  Pallas kernels  22.7 us (27%)
  other arithmetic  1 us (1%)
    ppermute x3, waiting for transfers between devices, packed_form(): lax.ppermute(parts[d], 'red', ring_z(d))  12.9 us
    pallas_call x2, Pallas kernels, packed_form(): pl.pallas_call(functools.partial(cycle_kernel, n_i, slots, first), grid=(...  8.24 us
    ppermute x3, waiting for transfers between devices, packed_form(): across = [mine] + [lax.ppermute(mine, 'blk', ring_x(d)) for d in (1, 2, 3)]  6.91 us
    ppermute x3, starting transfers between devices, packed_form(): lax.ppermute(parts[d], 'red', ring_z(d))  6.04 us
    ppermute x3, starting transfers between devices, over_y(): return [pb[0]] + [lax.ppermute(pb[d], 'blk', ring_y(d)) for d in (1, 2, 3)]  5.99 us
    ppermute x3, starting transfers between devices, packed_form(): across = [mine] + [lax.ppermute(mine, 'blk', ring_x(d)) for d in (1, 2, 3)]  5.72 us
    ppermute x3, waiting for transfers between devices, packed_form(): lax.ppermute(terms[d], 'blk', ring_y(RING - d))  5.61 us
    ppermute x3, starting transfers between devices, packed_form(): lax.ppermute(terms[d], 'blk', ring_y(RING - d))  4.68 us
  transfers between devices with their start and end apart: 17, of which 11 were waited for; matrix products, arithmetic and copies ran while one was open for 1% of the time, Pallas kernels for 15%

profile of v1, /device:TPU:0, one launch (start us, length us, event | category | flops | bytes accessed | tf_op | source)
XLA Modules:
  0.0 82.4 jit_solution(5218985218262680408)
XLA Ops:
  0.0 0.0 copy-start.2
  0.0 0.0 copy-start.3
  0.0 0.0 copy-start.5
  0.0 0.0 copy-start.4
  0.0 3.0 %pack_dressed.3 = (bf16[4,32,384]{2,1,0:T(8,128)(2,1)S(1)}, bf16[4,32,384]{2,1,0:T(8,128)(2,1)S(1)}, bf16[4,32,384]{2,1,0:T(8,128)(2,1)S(1)}, bf16[4,32,384]{2,1...) custom-call(s32[200]{0:T(256)} %occ_ref.3, s32[8]{0:T(128)} %sj_ref.1, s32[4]{0:T(128)} %sk_ref.3, ...), custom_call_target="tpu_custom_call" | custom-call | flops 536870912 | bytes 10485760 | tf_op jit(solution)/shard_map/pack_dressed/pallas_call | solution.py:478
  3.0 0.0 copy-start.6
  3.0 0.0 copy-start.7
  3.0 0.0 copy-start.8
  3.1 1.7 %collective-permute-start.29 = (bf16[4,32,384]{2,1,0:T(8,128)(2,1)S(1)}, bf16[4,32,384]{2,1,0:T(8,128)(2,1)S(1)}, u32[]{:S(2)}, u32[]{:S(2)}) collective-permute-start(bf16[4,32,384]{2,1,0:T(8,128)(2,1)S(1)} %get-tuple-element.198), channel_id=1, source_target_pairs={{0,8},{4,12},{8,16},{12,20},{16,24},{20,28},{24,0},{28,4},{32,40},... | collective-permute-start | bytes 294920 | tf_op jit(solution)/shard_map/ppermute | solution.py:551
  4.8 2.9 %collective-permute-start.30 = (bf16[4,32,384]{2,1,0:T(8,128)(2,1)S(1)}, bf16[4,32,384]{2,1,0:T(8,128)(2,1)}, u32[]{:S(2)}, u32[]{:S(2)}) collective-permute-start(bf16[4,32,384]{2,1,0:T(8,128)(2,1)S(1)} %get-tuple-element.199), channel_id=1, source_target_pairs={{0,16},{4,20},{8,24},{12,28},{16,0},{20,4},{24,8},{28,12},{32,48},... | collective-permute-start | bytes 294920 | tf_op jit(solution)/shard_map/ppermute | solution.py:551
  7.7 1.3 %collective-permute-start.31 = (bf16[4,32,384]{2,1,0:T(8,128)(2,1)S(1)}, bf16[4,32,384]{2,1,0:T(8,128)(2,1)}, u32[]{:S(2)}, u32[]{:S(2)}) collective-permute-start(bf16[4,32,384]{2,1,0:T(8,128)(2,1)S(1)} %get-tuple-element.200), channel_id=1, source_target_pairs={{0,24},{4,28},{8,0},{12,4},{16,8},{20,12},{24,16},{28,20},{32,56},... | collective-permute-start | bytes 294920 | tf_op jit(solution)/shard_map/ppermute | solution.py:551
  9.6 0.0 copy-done.2
  9.6 0.0 copy-done.3
  9.6 0.0 copy-done.5
  9.6 0.0 copy-done.4
  9.7 4.2 %pack_amplitudes.3 = bf16[4,4,10,32,128]{4,3,2,1,0:T(8,128)(2,1)} custom-call(s32[200]{0:T(256)S(1)} %copy-done.3, s32[8]{0:T(128)S(1)} %copy-done.4, s32[4]{0:T(128)S(1)} %copy-done.5, s32[1,1024]{1,0:T(1,128)S(1)} %bitcast.61, s32[1,1024]{1,0:T(1,128)S(1)} %get-tuple-element.201.rank_ref, bf16[4,8,32,1024]{3,2,1,0:T(8,128)(2,1)} %amp_ref.1), custom_call_target="tpu_custom_call" | custom-call | flops 536870912 | bytes 10485760 | tf_op jit(solution)/shard_map/pack_amplitudes/pallas_call | solution.py:503
  13.8 0.0 collective-permute-done.29
  13.8 0.0 collective-permute-done.30
  13.8 0.0 collective-permute-done.31
  13.8 0.0 copy-done.6
  13.8 0.0 copy-done.7
  13.9 0.0 copy-done.8
  13.9 68.5 %conditional.2 = (f32[8,8,32,256]{3,2,1,0:T(8,128)}) conditional(s32[]{:T(128)} %bitcast.32, (s32[1]{0:T(128)}, s32[8]{0:T(128)S(1)}, s32[200]{0:T(256)S(1)}, s32[8]{0:T(128)S(1)}, s32[1024]{0:T(1024)S(1)}, /*index=5*/bf16[8,8,32,256]{3,2,1,0:T(8,128)(2,1)}, (), s32[4]{0:T(128)S(1)}, bf16[4,8,32,1024]{3,2,1,0:T(8,128)(2,1)}, (), ...), branch_computations={%region_0.9_spmd, %region_9.10_spmd} | conditional | flops 17191471104 | bytes 320185760 | solution.py:690
  14.1 3.6 %all-to-all-start.1 = ((bf16[4,4,10,32,128]{4,3,2,1,0:T(8,128)(2,1)}), bf16[4,4,10,32,128]{4,3,2,1,0:T(8,128)(2,1)S(1)}, u32[]{:S(2)}, u32[]{:S(2)}) async-start(bf16[4,4,10,32,128]{4,3,2,1,0:T(8,128)(2,1)} %get-tuple-element.176), calls=%async_computation.1 | async-start | bytes 2621440 | tf_op jit(solution)/shard_map/cond/branch_1_fun/all_to_all | solution.py:583
  17.7 1.0 %pad_maximum_fusion.1.b0 = bf16[4,4,32,384]{3,2,1,0:T(8,128)(2,1)S(1)} fusion(bf16[1,4,32,384]{3,2,1,0:T(8,128)(2,1)} %bitcast.30, bf16[1,4,32,384]{3,2,1,0:T(8,128)(2,1)} %bitcast.29, bf16[1,4,32,384]{3,2,1,0:T(8,128)(2,1)S(1)} %bitcast.72, bf16[1,4,32,384]{3,2,1,0:T(8,128)(2,1)S(1)} %bitcast.71), kind=kLoop, calls=%fused_computation.3 | loop fusion | flops 589824 | bytes 786432 | tf_op jit(solution)/shard_map/cond/branch_1_fun/stack | solution.py:604
  18.7 1.6 %collective-permute-start.18 = (bf16[4,4,32,384]{3,2,1,0:T(8,128)(2,1)S(1)}, bf16[4,4,32,384]{3,2,1,0:T(8,128)(2,1)S(1)}, u32[]{:S(2)}, u32[]{:S(2)}) collective-permute-start(bf16[4,4,32,384]{3,2,1,0:T(8,128)(2,1)S(1)} %pad_maximum_fusion.1.b0), channel_id=1, source_target_pairs={{0,32},{4,36},{8,40},{12,44},{16,48},{20,52},{24,56},{28,60},{32,6... | collective-permute-start | bytes 1179656 | tf_op jit(solution)/shard_map/cond/branch_1_fun/ppermute | solution.py:605
  20.2 2.7 %collective-permute-start.16 = (bf16[4,4,32,384]{3,2,1,0:T(8,128)(2,1)S(1)}, bf16[4,4,32,384]{3,2,1,0:T(8,128)(2,1)S(1)}, u32[]{:S(2)}, u32[]{:S(2)}) collective-permute-start(bf16[4,4,32,384]{3,2,1,0:T(8,128)(2,1)S(1)} %pad_maximum_fusion.1.b0), channel_id=1, source_target_pairs={{0,64},{4,68},{8,72},{12,76},{16,80},{20,84},{24,88},{28,92},{32,9... | collective-permute-start | bytes 1179656 | tf_op jit(solution)/shard_map/cond/branch_1_fun/ppermute | solution.py:605
  23.0 1.4 %collective-permute-start.17 = (bf16[4,4,32,384]{3,2,1,0:T(8,128)(2,1)S(1)}, bf16[4,4,32,384]{3,2,1,0:T(8,128)(2,1)S(1)}, u32[]{:S(2)}, u32[]{:S(2)}) collective-permute-start(bf16[4,4,32,384]{3,2,1,0:T(8,128)(2,1)S(1)} %pad_maximum_fusion.1.b0), channel_id=1, source_target_pairs={{0,96},{4,100},{8,104},{12,108},{16,112},{20,116},{24,120},{28,124... | collective-permute-start | bytes 1179656 | tf_op jit(solution)/shard_map/cond/branch_1_fun/ppermute | solution.py:605
  24.4 0.0 collective-permute-start.19
  24.4 6.6 %collective-permute-done.18.b1 = bf16[4,4,32,384]{3,2,1,0:T(8,128)(2,1)S(1)} collective-permute-done((bf16[4,4,32,384]{3,2,1,0:T(8,128)(2,1)S(1)}, bf16[4,4,32,384]{3,2,1,0:T(8,128)(2,1)S(1)}, u32[]{:S(2)}, u32[]{:S(2)}) %collective-permute-start.18) | collective-permute-done | bytes 393248 | tf_op jit(solution)/shard_map/cond/branch_1_fun/ppermute | solution.py:605
  31.0 0.0 collective-permute-start.20
  31.0 4.0 %all-to-all-done.1.pa_ref = bf16[4,4,10,32,128]{4,3,2,1,0:T(8,128)(2,1)S(1)} async-done(((bf16[4,4,10,32,128]{4,3,2,1,0:T(8,128)(2,1)}), bf16[4,4,10,32,128]{4,3,2,1,0:T(8,128)(2,1)S(1)}, u32[]{:S(2)}, u32[]{:S(2)}) %all-to-all-start.1) | async-done | bytes 1310752 | tf_op jit(solution)/shard_map/cond/branch_1_fun/all_to_all | solution.py:583
  35.0 4.1 %unpack.3.a_ref = bf16[4,1024,1024]{2,1,0:T(8,128)(2,1)S(1)} custom-call(s32[200]{0:T(256)S(1)} %get-tuple-element.163.occ_ref, s32[8]{0:T(128)S(1)} %get-tuple-element.164.si_ref, s32[4]{0:T(128)S(1)} %get-tuple-element.174.sk_ref, s32[1,1024]{1,0:T(1,128)S(1)} %bitcast.66, s32[1,1024]{1,0:T(1,128)S(1)} %get-tuple-element.175.rank_ref, ...), custom_call_target="tpu_custom_call" | custom-call | flops 2147483648 | bytes 20971520 | tf_op jit(solution)/shard_map/cond/branch_1_fun/unpack/pallas_call | solution.py:586
  39.1 0.3 collective-permute-done.16.b2
  39.4 0.0 collective-permute-done.17.b3
  39.4 0.0 collective-permute-start.21
  39.4 0.5 collective-permute-start.22
  39.9 0.0 collective-permute-done.19.b4
  39.9 0.0 collective-permute-done.20.b5
  39.9 1.2 %collective-permute-done.21.b6 = bf16[4,4,32,384]{3,2,1,0:T(8,128)(2,1)S(1)} collective-permute-done((bf16[4,4,32,384]{3,2,1,0:T(8,128)(2,1)S(1)}, bf16[4,4,32,384]{3,2,1,0:T(8,128)(2,1)S(1)}, u32[]{:S(2)}, u32[]{:S(2)}) %collective-permute-start.21) | collective-permute-done | bytes 393248 | tf_op jit(solution)/shard_map/cond/branch_1_fun/ppermute | solution.py:607
  41.1 0.6 collective-permute-done.22.b7
  41.7 4.1 %cycle.7 = (f32[4,6,32,128]{3,2,1,0:T(8,128)S(1)}, f32[4,6,32,128]{3,2,1,0:T(8,128)S(1)}) custom-call(bf16[4,1024,1024]{2,1,0:T(8,128)(2,1)S(1)} %unpack.3.a_ref, bf16[4,4,32,384]{3,2,1,0:T(8,128)(2,1)S(1)} %pad_maximum_fusion.1.b0, bf16[4,4,32,384]{3,2,1,0:T(8,128)(2,1)S(1)} %collective-permute-done.18.b1, ...), custom_call_target="tpu_custom_call" | custom-call | flops 2147483648 | bytes 14680064 | tf_op jit(solution)/shard_map/cond/branch_1_fun/cycle/pallas_call | solution.py:610
  45.8 2.0 %collective-permute-start.23 = (f32[4,6,32,128]{3,2,1,0:T(8,128)S(1)}, f32[4,6,32,128]{3,2,1,0:T(8,128)S(1)}, u32[]{:S(2)}, u32[]{:S(2)}) collective-permute-start(f32[4,6,32,128]{3,2,1,0:T(8,128)S(1)} %get-tuple-element.181), channel_id=1, source_target_pairs={{0,1},{1,2},{2,3},{3,0},{4,5},{5,6},{6,7},{7,4},{8,9},{9,10},{10,1... | collective-permute-start | bytes 1179656 | tf_op jit(solution)/shard_map/cond/branch_1_fun/ppermute | solution.py:623
  47.7 2.2 %collective-permute-start.25 = (f32[4,6,32,128]{3,2,1,0:T(8,128)S(1)}, f32[4,6,32,128]{3,2,1,0:T(8,128)S(1)}, u32[]{:S(2)}, u32[]{:S(2)}) collective-permute-start(f32[4,6,32,128]{3,2,1,0:T(8,128)S(1)} %get-tuple-element.183), channel_id=1, source_target_pairs={{0,3},{1,0},{2,1},{3,2},{4,7},{5,4},{6,5},{7,6},{8,11},{9,8},{10,9... | collective-permute-start | bytes 1179656 | tf_op jit(solution)/shard_map/cond/branch_1_fun/ppermute | solution.py:623
  49.9 4.2 %cycle.6 = (f32[4,6,32,128]{3,2,1,0:T(8,128)S(1)}, f32[4,6,32,128]{3,2,1,0:T(8,128)S(1)}) custom-call(bf16[4,1024,1024]{2,1,0:T(8,128)(2,1)S(1)} %unpack.3.a_ref, bf16[4,4,32,384]{3,2,1,0:T(8,128)(2,1)S(1)} %pad_maximum_fusion.1.b0, bf16[4,4,32,384]{3,2,1,0:T(8,128)(2,1)S(1)} %collective-permute-done.18.b1, ...), custom_call_target="tpu_custom_call" | custom-call | flops 2147483648 | bytes 14680064 | tf_op jit(solution)/shard_map/cond/branch_1_fun/cycle/pallas_call | solution.py:610
  54.1 0.0 copy-start.1
  54.1 1.9 %collective-permute-start.24 = (f32[4,6,32,128]{3,2,1,0:T(8,128)S(1)}, f32[4,6,32,128]{3,2,1,0:T(8,128)S(1)}, u32[]{:S(2)}, u32[]{:S(2)}) collective-permute-start(f32[4,6,32,128]{3,2,1,0:T(8,128)S(1)} %get-tuple-element.182), channel_id=1, source_target_pairs={{0,2},{1,3},{2,0},{3,1},{4,6},{5,7},{6,4},{7,5},{8,10},{9,11},{10,... | collective-permute-start | bytes 1179656 | tf_op jit(solution)/shard_map/cond/branch_1_fun/ppermute | solution.py:623
  56.0 3.3 %collective-permute-done.23.o1 = f32[4,6,32,128]{3,2,1,0:T(8,128)S(1)} collective-permute-done((f32[4,6,32,128]{3,2,1,0:T(8,128)S(1)}, f32[4,6,32,128]{3,2,1,0:T(8,128)S(1)}, u32[]{:S(2)}, u32[]{:S(2)}) %collective-permute-start.23) | collective-permute-done | bytes 393248 | tf_op jit(solution)/shard_map/cond/branch_1_fun/ppermute | solution.py:623
  59.3 7.8 %collective-permute-done.25.o3 = f32[4,6,32,128]{3,2,1,0:T(8,128)S(1)} collective-permute-done((f32[4,6,32,128]{3,2,1,0:T(8,128)S(1)}, f32[4,6,32,128]{3,2,1,0:T(8,128)S(1)}, u32[]{:S(2)}, u32[]{:S(2)}) %collective-permute-start.25) | collective-permute-done | bytes 393248 | tf_op jit(solution)/shard_map/cond/branch_1_fun/ppermute | solution.py:623
  67.1 1.8 %collective-permute-done.24.o2 = f32[4,6,32,128]{3,2,1,0:T(8,128)S(1)} collective-permute-done((f32[4,6,32,128]{3,2,1,0:T(8,128)S(1)}, f32[4,6,32,128]{3,2,1,0:T(8,128)S(1)}, u32[]{:S(2)}, u32[]{:S(2)}) %collective-permute-start.24) | collective-permute-done | bytes 393248 | tf_op jit(solution)/shard_map/cond/branch_1_fun/ppermute | solution.py:623
  68.9 0.2 sums.3
  69.1 3.0 %collective-permute-start.26 = (f32[6,32,128]{2,1,0:T(8,128)S(1)}, f32[6,32,128]{2,1,0:T(8,128)S(1)}, u32[]{:S(2)}, u32[]{:S(2)}) collective-permute-start(f32[6,32,128]{2,1,0:T(8,128)S(1)} %get-tuple-element.185), channel_id=1, source_target_pairs={{0,24},{4,28},{8,0},{12,4},{16,8},{20,12},{24,16},{28,20},{32,56},... | collective-permute-start | bytes 294920 | tf_op jit(solution)/shard_map/cond/branch_1_fun/ppermute | solution.py:634
  72.1 0.9 %collective-permute-start.27 = (f32[6,32,128]{2,1,0:T(8,128)S(1)}, f32[6,32,128]{2,1,0:T(8,128)S(1)}, u32[]{:S(2)}, u32[]{:S(2)}) collective-permute-start(f32[6,32,128]{2,1,0:T(8,128)S(1)} %get-tuple-element.186), channel_id=1, source_target_pairs={{0,16},{4,20},{8,24},{12,28},{16,0},{20,4},{24,8},{28,12},{32,48},... | collective-permute-start | bytes 294920 | tf_op jit(solution)/shard_map/cond/branch_1_fun/ppermute | solution.py:634
  73.0 0.8 %collective-permute-start.28 = (f32[6,32,128]{2,1,0:T(8,128)S(1)}, f32[6,32,128]{2,1,0:T(8,128)S(1)}, u32[]{:S(2)}, u32[]{:S(2)}) collective-permute-start(f32[6,32,128]{2,1,0:T(8,128)S(1)} %get-tuple-element.187), channel_id=1, source_target_pairs={{0,8},{4,12},{8,16},{12,20},{16,24},{20,28},{24,0},{28,4},{32,40},... | collective-permute-start | bytes 294920 | tf_op jit(solution)/shard_map/cond/branch_1_fun/ppermute | solution.py:634
  73.8 2.1 %collective-permute-done.26.t1 = f32[6,32,128]{2,1,0:T(8,128)S(1)} collective-permute-done((f32[6,32,128]{2,1,0:T(8,128)S(1)}, f32[6,32,128]{2,1,0:T(8,128)S(1)}, u32[]{:S(2)}, u32[]{:S(2)}) %collective-permute-start.26) | collective-permute-done | bytes 98336 | tf_op jit(solution)/shard_map/cond/branch_1_fun/ppermute | solution.py:634
  76.0 2.5 %collective-permute-done.27.t2 = f32[6,32,128]{2,1,0:T(8,128)S(1)} collective-permute-done((f32[6,32,128]{2,1,0:T(8,128)S(1)}, f32[6,32,128]{2,1,0:T(8,128)S(1)}, u32[]{:S(2)}, u32[]{:S(2)}) %collective-permute-start.27) | collective-permute-done | bytes 98336 | tf_op jit(solution)/shard_map/cond/branch_1_fun/ppermute | solution.py:634
  78.4 1.0 %collective-permute-done.28.t3 = f32[6,32,128]{2,1,0:T(8,128)S(1)} collective-permute-done((f32[6,32,128]{2,1,0:T(8,128)S(1)}, f32[6,32,128]{2,1,0:T(8,128)S(1)}, u32[]{:S(2)}, u32[]{:S(2)}) %collective-permute-start.28) | collective-permute-done | bytes 98336 | tf_op jit(solution)/shard_map/cond/branch_1_fun/ppermute | solution.py:634
  79.4 0.0 copy-done.1
  79.4 2.9 %update.3 = f32[8,8,32,256]{3,2,1,0:T(8,128)} custom-call(s32[200]{0:T(256)S(1)} %get-tuple-element.163.occ_ref, s32[8]{0:T(128)S(1)} %get-tuple-element.164.si_ref, s32[8]{0:T(128)S(1)} %get-tuple-element.165.sj_ref, f32[200]{0:T(256)S(1)} %get-tuple-element.166.oe_ref, s32[1,1024]{1,0:T(1,128)S(1)} %bitcast.67, f32[1,1024]{1,0:T(1,128)S(1)} %bitcast.74, ...), custom_call_target="tpu_custom_call" | custom-call | flops 402653184 | bytes 4194304 | tf_op jit(solution)/shard_map/cond/branch_1_fun/update/pallas_call | solution.py:636
Async XLA Ops:
  0.0 9.6 %copy-start.2 = (s32[1024]{0:T(1024)S(1)}, s32[1024]{0:T(1024)}, u32[]{:S(2)}) copy-start(s32[1024]{0:T(1024)} %param.20) | copy-start | bytes 12292
  0.0 9.6 %copy-start.3 = (s32[200]{0:T(256)S(1)}, s32[200]{0:T(256)}, u32[]{:S(2)}) copy-start(s32[200]{0:T(256)} %occ_ref.3) | copy-start | bytes 2404
  0.0 9.6 %copy-start.5 = (s32[4]{0:T(128)S(1)}, s32[4]{0:T(128)}, u32[]{:S(2)}) copy-start(s32[4]{0:T(128)} %sk_ref.3) | copy-start | bytes 52
  0.0 9.6 %copy-start.4 = (s32[8]{0:T(128)S(1)}, s32[8]{0:T(128)}, u32[]{:S(2)}) copy-start(s32[8]{0:T(128)} %si_ref.1) | copy-start | bytes 100
  3.0 10.8 %copy-start.6 = (f32[1024]{0:T(1024)S(1)}, f32[1024]{0:T(1024)}, u32[]{:S(2)}) copy-start(f32[1024]{0:T(1024)} %param.22) | copy-start | bytes 12292
  3.0 10.8 %copy-start.7 = (s32[8]{0:T(128)S(1)}, s32[8]{0:T(128)}, u32[]{:S(2)}) copy-start(s32[8]{0:T(128)} %sj_ref.1) | copy-start | bytes 100
  3.0 10.8 %copy-start.8 = (f32[200]{0:T(256)S(1)}, f32[200]{0:T(256)}, u32[]{:S(2)}) copy-start(f32[200]{0:T(256)} %param.21) | copy-start | bytes 2404
  3.1 10.8 %collective-permute-start.29 = (bf16[4,32,384]{2,1,0:T(8,128)(2,1)S(1)}, bf16[4,32,384]{2,1,0:T(8,128)(2,1)S(1)}, u32[]{:S(2)}, u32[]{:S(2)}) collective-permute-start(bf16[4,32,384]{2,1,0:T(8,128)(2,1)S(1)} %get-tuple-element.198), channel_id=1, source_target_pairs={{0,8},{4,12},{8,16},{12,20},{16,24},{20,28},{24,0},{28,4},{32,40},... | collective-permute-start | bytes 294920 | tf_op jit(solution)/shard_map/ppermute | solution.py:551
  4.8 9.0 %collective-permute-start.30 = (bf16[4,32,384]{2,1,0:T(8,128)(2,1)S(1)}, bf16[4,32,384]{2,1,0:T(8,128)(2,1)}, u32[]{:S(2)}, u32[]{:S(2)}) collective-permute-start(bf16[4,32,384]{2,1,0:T(8,128)(2,1)S(1)} %get-tuple-element.199), channel_id=1, source_target_pairs={{0,16},{4,20},{8,24},{12,28},{16,0},{20,4},{24,8},{28,12},{32,48},... | collective-permute-start | bytes 294920 | tf_op jit(solution)/shard_map/ppermute | solution.py:551
  7.7 6.1 %collective-permute-start.31 = (bf16[4,32,384]{2,1,0:T(8,128)(2,1)S(1)}, bf16[4,32,384]{2,1,0:T(8,128)(2,1)}, u32[]{:S(2)}, u32[]{:S(2)}) collective-permute-start(bf16[4,32,384]{2,1,0:T(8,128)(2,1)S(1)} %get-tuple-element.200), channel_id=1, source_target_pairs={{0,24},{4,28},{8,0},{12,4},{16,8},{20,12},{24,16},{28,20},{32,56},... | collective-permute-start | bytes 294920 | tf_op jit(solution)/shard_map/ppermute | solution.py:551
  14.1 20.9 %all-to-all-start.1 = ((bf16[4,4,10,32,128]{4,3,2,1,0:T(8,128)(2,1)}), bf16[4,4,10,32,128]{4,3,2,1,0:T(8,128)(2,1)S(1)}, u32[]{:S(2)}, u32[]{:S(2)}) async-start(bf16[4,4,10,32,128]{4,3,2,1,0:T(8,128)(2,1)} %get-tuple-element.176), calls=%async_computation.1 | async-start | bytes 2621440 | tf_op jit(solution)/shard_map/cond/branch_1_fun/all_to_all | solution.py:583
  18.7 12.3 %collective-permute-start.18 = (bf16[4,4,32,384]{3,2,1,0:T(8,128)(2,1)S(1)}, bf16[4,4,32,384]{3,2,1,0:T(8,128)(2,1)S(1)}, u32[]{:S(2)}, u32[]{:S(2)}) collective-permute-start(bf16[4,4,32,384]{3,2,1,0:T(8,128)(2,1)S(1)} %pad_maximum_fusion.1.b0), channel_id=1, source_target_pairs={{0,32},{4,36},{8,40},{12,44},{16,48},{20,52},{24,56},{28,60},{32,6... | collective-permute-start | bytes 1179656 | tf_op jit(solution)/shard_map/cond/branch_1_fun/ppermute | solution.py:605
  20.2 19.1 %collective-permute-start.16 = (bf16[4,4,32,384]{3,2,1,0:T(8,128)(2,1)S(1)}, bf16[4,4,32,384]{3,2,1,0:T(8,128)(2,1)S(1)}, u32[]{:S(2)}, u32[]{:S(2)}) collective-permute-start(bf16[4,4,32,384]{3,2,1,0:T(8,128)(2,1)S(1)} %pad_maximum_fusion.1.b0), channel_id=1, source_target_pairs={{0,64},{4,68},{8,72},{12,76},{16,80},{20,84},{24,88},{28,92},{32,9... | collective-permute-start | bytes 1179656 | tf_op jit(solution)/shard_map/cond/branch_1_fun/ppermute | solution.py:605
  23.0 16.4 %collective-permute-start.17 = (bf16[4,4,32,384]{3,2,1,0:T(8,128)(2,1)S(1)}, bf16[4,4,32,384]{3,2,1,0:T(8,128)(2,1)S(1)}, u32[]{:S(2)}, u32[]{:S(2)}) collective-permute-start(bf16[4,4,32,384]{3,2,1,0:T(8,128)(2,1)S(1)} %pad_maximum_fusion.1.b0), channel_id=1, source_target_pairs={{0,96},{4,100},{8,104},{12,108},{16,112},{20,116},{24,120},{28,124... | collective-permute-start | bytes 1179656 | tf_op jit(solution)/shard_map/cond/branch_1_fun/ppermute | solution.py:605
  24.4 15.5 %collective-permute-start.19 = (bf16[4,4,32,384]{3,2,1,0:T(8,128)(2,1)S(1)}, bf16[4,4,32,384]{3,2,1,0:T(8,128)(2,1)S(1)}, u32[]{:S(2)}, u32[]{:S(2)}) collective-permute-start(bf16[4,4,32,384]{3,2,1,0:T(8,128)(2,1)S(1)} %pad_maximum_fusion.1.b0), channel_id=1, source_target_pairs={{0,4},{4,0},{8,12},{12,8},{16,20},{20,16},{24,28},{28,24},{32,36},... | collective-permute-start | bytes 1179656 | tf_op jit(solution)/shard_map/cond/branch_1_fun/ppermute | solution.py:607
  31.0 8.9 %collective-permute-start.20 = (bf16[4,4,32,384]{3,2,1,0:T(8,128)(2,1)S(1)}, bf16[4,4,32,384]{3,2,1,0:T(8,128)(2,1)}, u32[]{:S(2)}, u32[]{:S(2)}) collective-permute-start(bf16[4,4,32,384]{3,2,1,0:T(8,128)(2,1)S(1)} %collective-permute-done.18.b1), channel_id=1, source_target_pairs={{0,4},{4,0},{8,12},{12,8},{16,20},{20,16},{24,28},{28,24},{32,36},... | collective-permute-start | bytes 1179656 | tf_op jit(solution)/shard_map/cond/branch_1_fun/ppermute | solution.py:607
  39.4 1.7 %collective-permute-start.21 = (bf16[4,4,32,384]{3,2,1,0:T(8,128)(2,1)S(1)}, bf16[4,4,32,384]{3,2,1,0:T(8,128)(2,1)S(1)}, u32[]{:S(2)}, u32[]{:S(2)}) collective-permute-start(bf16[4,4,32,384]{3,2,1,0:T(8,128)(2,1)S(1)} %collective-permute-done.16.b2), channel_id=1, source_target_pairs={{0,4},{4,0},{8,12},{12,8},{16,20},{20,16},{24,28},{28,24},{32,36},... | collective-permute-start | bytes 1179656 | tf_op jit(solution)/shard_map/cond/branch_1_fun/ppermute | solution.py:607
  39.4 2.3 %collective-permute-start.22 = (bf16[4,4,32,384]{3,2,1,0:T(8,128)(2,1)S(1)}, bf16[4,4,32,384]{3,2,1,0:T(8,128)(2,1)S(1)}, u32[]{:S(2)}, u32[]{:S(2)}) collective-permute-start(bf16[4,4,32,384]{3,2,1,0:T(8,128)(2,1)S(1)} %collective-permute-done.17.b3), channel_id=1, source_target_pairs={{0,4},{4,0},{8,12},{12,8},{16,20},{20,16},{24,28},{28,24},{32,36},... | collective-permute-start | bytes 1179656 | tf_op jit(solution)/shard_map/cond/branch_1_fun/ppermute | solution.py:607
  45.8 13.5 %collective-permute-start.23 = (f32[4,6,32,128]{3,2,1,0:T(8,128)S(1)}, f32[4,6,32,128]{3,2,1,0:T(8,128)S(1)}, u32[]{:S(2)}, u32[]{:S(2)}) collective-permute-start(f32[4,6,32,128]{3,2,1,0:T(8,128)S(1)} %get-tuple-element.181), channel_id=1, source_target_pairs={{0,1},{1,2},{2,3},{3,0},{4,5},{5,6},{6,7},{7,4},{8,9},{9,10},{10,1... | collective-permute-start | bytes 1179656 | tf_op jit(solution)/shard_map/cond/branch_1_fun/ppermute | solution.py:623
  47.7 19.4 %collective-permute-start.25 = (f32[4,6,32,128]{3,2,1,0:T(8,128)S(1)}, f32[4,6,32,128]{3,2,1,0:T(8,128)S(1)}, u32[]{:S(2)}, u32[]{:S(2)}) collective-permute-start(f32[4,6,32,128]{3,2,1,0:T(8,128)S(1)} %get-tuple-element.183), channel_id=1, source_target_pairs={{0,3},{1,0},{2,1},{3,2},{4,7},{5,4},{6,5},{7,6},{8,11},{9,8},{10,9... | collective-permute-start | bytes 1179656 | tf_op jit(solution)/shard_map/cond/branch_1_fun/ppermute | solution.py:623
  54.1 25.3 %copy-start.1 = (bf16[8,8,32,256]{3,2,1,0:T(8,128)(2,1)S(1)}, bf16[8,8,32,256]{3,2,1,0:T(8,128)(2,1)}, u32[]{:S(2)}) copy-start(bf16[8,8,32,256]{3,2,1,0:T(8,128)(2,1)} %get-tuple-element.188.int_ref) | copy-start | bytes 3145732 | tf_op jit(solution)/shard_map/cond
  54.1 14.8 %collective-permute-start.24 = (f32[4,6,32,128]{3,2,1,0:T(8,128)S(1)}, f32[4,6,32,128]{3,2,1,0:T(8,128)S(1)}, u32[]{:S(2)}, u32[]{:S(2)}) collective-permute-start(f32[4,6,32,128]{3,2,1,0:T(8,128)S(1)} %get-tuple-element.182), channel_id=1, source_target_pairs={{0,2},{1,3},{2,0},{3,1},{4,6},{5,7},{6,4},{7,5},{8,10},{9,11},{10,... | collective-permute-start | bytes 1179656 | tf_op jit(solution)/shard_map/cond/branch_1_fun/ppermute | solution.py:623
  69.1 6.8 %collective-permute-start.26 = (f32[6,32,128]{2,1,0:T(8,128)S(1)}, f32[6,32,128]{2,1,0:T(8,128)S(1)}, u32[]{:S(2)}, u32[]{:S(2)}) collective-permute-start(f32[6,32,128]{2,1,0:T(8,128)S(1)} %get-tuple-element.185), channel_id=1, source_target_pairs={{0,24},{4,28},{8,0},{12,4},{16,8},{20,12},{24,16},{28,20},{32,56},... | collective-permute-start | bytes 294920 | tf_op jit(solution)/shard_map/cond/branch_1_fun/ppermute | solution.py:634
  72.1 6.3 %collective-permute-start.27 = (f32[6,32,128]{2,1,0:T(8,128)S(1)}, f32[6,32,128]{2,1,0:T(8,128)S(1)}, u32[]{:S(2)}, u32[]{:S(2)}) collective-permute-start(f32[6,32,128]{2,1,0:T(8,128)S(1)} %get-tuple-element.186), channel_id=1, source_target_pairs={{0,16},{4,20},{8,24},{12,28},{16,0},{20,4},{24,8},{28,12},{32,48},... | collective-permute-start | bytes 294920 | tf_op jit(solution)/shard_map/cond/branch_1_fun/ppermute | solution.py:634
  73.0 6.5 %collective-permute-start.28 = (f32[6,32,128]{2,1,0:T(8,128)S(1)}, f32[6,32,128]{2,1,0:T(8,128)S(1)}, u32[]{:S(2)}, u32[]{:S(2)}) collective-permute-start(f32[6,32,128]{2,1,0:T(8,128)S(1)} %get-tuple-element.187), channel_id=1, source_target_pairs={{0,8},{4,12},{8,16},{12,20},{16,24},{20,28},{24,0},{28,4},{32,40},... | collective-permute-start | bytes 294920 | tf_op jit(solution)/shard_map/cond/branch_1_fun/ppermute | solution.py:634

commit v2 on v1

--- a/solution.py
+++ b/solution.py
@@ -548,7 +548,7 @@
 
 
 def over_y(pb):
-    return [pb[0]] + [lax.ppermute(pb[d], "blk", ring_y(d)) for d in (1, 2, 3)]
+    return jnp.stack([pb[0]] + [lax.ppermute(pb[d], "blk", ring_y(d)) for d in (1, 2, 3)])
 
 
 def packed_form(
@@ -601,7 +601,7 @@
         name="unpack",
     )(occ_irrep, slab_i, slab_k, lv, rank, pa_y)
 
-    mine = jnp.stack(pb_y)
+    mine = pb_y
     across = [mine] + [lax.ppermute(mine, "blk", ring_x(d)) for d in (1, 2, 3)]
     *across[2:], spread = lax.optimization_barrier((*across[2:], spread))
     twin = [lax.ppermute(b, "blk", other_core()) for b in across]

time: 82.7 us -> 82.6 us (level)
  transfers between devices with their start and end apart: 17 -> 17, of which waited for: 11 -> 10; matrix products, arithmetic and copies ran while one was open for 1% -> 0% of each run, Pallas kernels for 15% -> 15%
where the time goes in v2:
time: 82.6 us; the launch traced here: 82.3 us
  waiting for transfers between devices  32 us (39%)
  starting transfers between devices  26 us (31%)
  Pallas kernels  22.4 us (27%)
  other arithmetic  0.84 us (1%)
    ppermute x3, waiting for transfers between devices, packed_form(): lax.ppermute(parts[d], 'red', ring_z(d))  13 us
    pallas_call x2, Pallas kernels, packed_form(): pl.pallas_call(functools.partial(cycle_kernel, n_i, slots, first), grid=(...  7.99 us
    ppermute x3, waiting for transfers between devices, packed_form(): across = [mine] + [lax.ppermute(mine, 'blk', ring_x(d)) for d in (1, 2, 3)]  6.81 us
    ppermute x3, starting transfers between devices, packed_form(): lax.ppermute(parts[d], 'red', ring_z(d))  6.07 us
    ppermute x3, starting transfers between devices, over_y(): lax.ppermute(pb[d], 'blk', ring_y(d))  5.99 us
    ppermute x3, starting transfers between devices, packed_form(): across = [mine] + [lax.ppermute(mine, 'blk', ring_x(d)) for d in (1, 2, 3)]  5.74 us
    ppermute x3, waiting for transfers between devices, packed_form(): lax.ppermute(terms[d], 'blk', ring_y(RING - d))  5.64 us
    all_to_all x1, waiting for transfers between devices, packed_form(): pa_y = lax.all_to_all(pa, 'blk', 0, 0, axis_index_groups=groups_y())  4.76 us
  transfers between devices with their start and end apart: 17, of which 10 were waited for; matrix products, arithmetic and copies ran while one was open for 0% of the time, Pallas kernels for 15%

profile of v2, /device:TPU:0, one launch (start us, length us, event | category | flops | bytes accessed | tf_op | source)
XLA Modules:
  0.0 82.3 jit_solution(10334345688049793419)
XLA Ops:
  0.0 0.0 copy-start.2
  0.0 0.0 copy-start.3
  0.0 0.0 copy-start.5
  0.0 0.0 copy-start.4
  0.0 3.0 %pack_dressed.3 = (bf16[4,32,384]{2,1,0:T(8,128)(2,1)S(1)}, bf16[4,32,384]{2,1,0:T(8,128)(2,1)S(1)}, bf16[4,32,384]{2,1,0:T(8,128)(2,1)S(1)}, bf16[4,32,384]{2,1...) custom-call(s32[200]{0:T(256)} %occ_ref.3, s32[8]{0:T(128)} %sj_ref.1, s32[4]{0:T(128)} %sk_ref.3, ...), custom_call_target="tpu_custom_call" | custom-call | flops 536870912 | bytes 10485760 | tf_op jit(solution)/shard_map/pack_dressed/pallas_call | solution.py:478
  3.0 1.7 %collective-permute-start.29 = (bf16[4,32,384]{2,1,0:T(8,128)(2,1)S(1)}, bf16[4,32,384]{2,1,0:T(8,128)(2,1)S(1)}, u32[]{:S(2)}, u32[]{:S(2)}) collective-permute-start(bf16[4,32,384]{2,1,0:T(8,128)(2,1)S(1)} %get-tuple-element.189), channel_id=1, source_target_pairs={{0,8},{4,12},{8,16},{12,20},{16,24},{20,28},{24,0},{28,4},{32,40},... | collective-permute-start | bytes 294920 | tf_op jit(solution)/shard_map/ppermute | solution.py:551
  4.8 2.9 %collective-permute-start.30 = (bf16[4,32,384]{2,1,0:T(8,128)(2,1)S(1)}, bf16[4,32,384]{2,1,0:T(8,128)(2,1)S(1)}, u32[]{:S(2)}, u32[]{:S(2)}) collective-permute-start(bf16[4,32,384]{2,1,0:T(8,128)(2,1)S(1)} %get-tuple-element.190), channel_id=1, source_target_pairs={{0,16},{4,20},{8,24},{12,28},{16,0},{20,4},{24,8},{28,12},{32,48},... | collective-permute-start | bytes 294920 | tf_op jit(solution)/shard_map/ppermute | solution.py:551
  7.7 1.3 %collective-permute-start.31 = (bf16[4,32,384]{2,1,0:T(8,128)(2,1)S(1)}, bf16[4,32,384]{2,1,0:T(8,128)(2,1)S(1)}, u32[]{:S(2)}, u32[]{:S(2)}) collective-permute-start(bf16[4,32,384]{2,1,0:T(8,128)(2,1)S(1)} %get-tuple-element.191), channel_id=1, source_target_pairs={{0,24},{4,28},{8,0},{12,4},{16,8},{20,12},{24,16},{28,20},{32,56},... | collective-permute-start | bytes 294920 | tf_op jit(solution)/shard_map/ppermute | solution.py:551
  9.7 0.0 copy-done.2
  9.7 0.0 copy-done.3
  9.7 0.0 copy-done.5
  9.7 0.0 copy-done.4
  9.7 0.0 copy-start.6
  9.8 0.0 copy-start.7
  9.8 0.0 copy-start.8
  9.8 4.1 %pack_amplitudes.3 = bf16[4,4,10,32,128]{4,3,2,1,0:T(8,128)(2,1)} custom-call(s32[200]{0:T(256)S(1)} %copy-done.3, s32[8]{0:T(128)S(1)} %copy-done.4, s32[4]{0:T(128)S(1)} %copy-done.5, s32[1,1024]{1,0:T(1,128)S(1)} %bitcast.62, s32[1,1024]{1,0:T(1,128)S(1)} %get-tuple-element.192.rank_ref, bf16[4,8,32,1024]{3,2,1,0:T(8,128)(2,1)} %amp_ref.1), custom_call_target="tpu_custom_call" | custom-call | flops 536870912 | bytes 10485760 | tf_op jit(solution)/shard_map/pack_amplitudes/pallas_call | solution.py:503
  13.9 0.0 collective-permute-done.29
  13.9 0.0 collective-permute-done.30
  13.9 0.0 collective-permute-done.31
  13.9 0.8 %pad_maximum_fusion.1 = bf16[4,4,32,384]{3,2,1,0:T(8,128)(2,1)} fusion(bf16[1,4,32,384]{3,2,1,0:T(8,128)(2,1)S(1)} %bitcast.74, bf16[1,4,32,384]{3,2,1,0:T(8,128)(2,1)S(1)} %bitcast.73, bf16[1,4,32,384]{3,2,1,0:T(8,128)(2,1)S(1)} %bitcast.72, bf16[1,4,32,384]{3,2,1,0:T(8,128)(2,1)S(1)} %bitcast.53), kind=kLoop, calls=%fused_computation.28 | loop fusion | flops 589824 | bytes 786432 | tf_op jit(solution)/shard_map/stack | solution.py:551
  14.8 0.0 copy-done.6
  14.8 0.0 copy-done.7
  14.8 0.0 copy-done.8
  14.8 67.5 %conditional.2 = (f32[8,8,32,256]{3,2,1,0:T(8,128)}) conditional(s32[]{:T(128)} %bitcast.28, (s32[1]{0:T(128)}, s32[8]{0:T(128)S(1)}, s32[200]{0:T(256)S(1)}, s32[8]{0:T(128)S(1)}, s32[1024]{0:T(1024)S(1)}, /*index=5*/bf16[8,8,32,256]{3,2,1,0:T(8,128)(2,1)}, (), s32[4]{0:T(128)S(1)}, bf16[4,8,32,1024]{3,2,1,0:T(8,128)(2,1)}, (), ...), branch_computations={%region_0.9_spmd, %region_9.10_spmd} | conditional | flops 17191471104 | bytes 320185760 | solution.py:690
  15.0 3.6 %all-to-all-start = ((bf16[4,4,10,32,128]{4,3,2,1,0:T(8,128)(2,1)}), bf16[4,4,10,32,128]{4,3,2,1,0:T(8,128)(2,1)S(1)}, u32[]{:S(2)}, u32[]{:S(2)}) async-start(bf16[4,4,10,32,128]{4,3,2,1,0:T(8,128)(2,1)} %get-tuple-element.167), calls=%async_computation | async-start | bytes 2621440 | tf_op jit(solution)/shard_map/cond/branch_1_fun/all_to_all | solution.py:583
  18.6 1.6 %collective-permute-start.2 = (bf16[4,4,32,384]{3,2,1,0:T(8,128)(2,1)}, bf16[4,4,32,384]{3,2,1,0:T(8,128)(2,1)S(1)}, u32[]{:S(2)}, u32[]{:S(2)}) collective-permute-start(bf16[4,4,32,384]{3,2,1,0:T(8,128)(2,1)} %get-tuple-element.164.b0), channel_id=1, source_target_pairs={{0,32},{4,36},{8,40},{12,44},{16,48},{20,52},{24,56},{28,60},{32,6... | collective-permute-start | bytes 1179656 | tf_op jit(solution)/shard_map/cond/branch_1_fun/ppermute | solution.py:605
  20.2 2.7 %collective-permute-start = (bf16[4,4,32,384]{3,2,1,0:T(8,128)(2,1)}, bf16[4,4,32,384]{3,2,1,0:T(8,128)(2,1)S(1)}, u32[]{:S(2)}, u32[]{:S(2)}) collective-permute-start(bf16[4,4,32,384]{3,2,1,0:T(8,128)(2,1)} %get-tuple-element.164.b0), channel_id=1, source_target_pairs={{0,64},{4,68},{8,72},{12,76},{16,80},{20,84},{24,88},{28,92},{32,9... | collective-permute-start | bytes 1179656 | tf_op jit(solution)/shard_map/cond/branch_1_fun/ppermute | solution.py:605
  22.9 1.4 %collective-permute-start.1 = (bf16[4,4,32,384]{3,2,1,0:T(8,128)(2,1)}, bf16[4,4,32,384]{3,2,1,0:T(8,128)(2,1)S(1)}, u32[]{:S(2)}, u32[]{:S(2)}) collective-permute-start(bf16[4,4,32,384]{3,2,1,0:T(8,128)(2,1)} %get-tuple-element.164.b0), channel_id=1, source_target_pairs={{0,96},{4,100},{8,104},{12,108},{16,112},{20,116},{24,120},{28,124... | collective-permute-start | bytes 1179656 | tf_op jit(solution)/shard_map/cond/branch_1_fun/ppermute | solution.py:605
  24.3 0.0 collective-permute-start.3
  24.3 6.8 %collective-permute-done.2.b1 = bf16[4,4,32,384]{3,2,1,0:T(8,128)(2,1)S(1)} collective-permute-done((bf16[4,4,32,384]{3,2,1,0:T(8,128)(2,1)}, bf16[4,4,32,384]{3,2,1,0:T(8,128)(2,1)S(1)}, u32[]{:S(2)}, u32[]{:S(2)}) %collective-permute-start.2) | collective-permute-done | bytes 393248 | tf_op jit(solution)/shard_map/cond/branch_1_fun/ppermute | solution.py:605
  31.1 0.0 collective-permute-start.4
  31.1 4.8 %all-to-all-done.pa_ref = bf16[4,4,10,32,128]{4,3,2,1,0:T(8,128)(2,1)S(1)} async-done(((bf16[4,4,10,32,128]{4,3,2,1,0:T(8,128)(2,1)}), bf16[4,4,10,32,128]{4,3,2,1,0:T(8,128)(2,1)S(1)}, u32[]{:S(2)}, u32[]{:S(2)}) %all-to-all-start) | async-done | bytes 1310752 | tf_op jit(solution)/shard_map/cond/branch_1_fun/all_to_all | solution.py:583
  35.9 4.1 %unpack.3.a_ref = bf16[4,1024,1024]{2,1,0:T(8,128)(2,1)S(1)} custom-call(s32[200]{0:T(256)S(1)} %get-tuple-element.157.occ_ref, s32[8]{0:T(128)S(1)} %get-tuple-element.158.si_ref, s32[4]{0:T(128)S(1)} %get-tuple-element.165.sk_ref, s32[1,1024]{1,0:T(1,128)S(1)} %bitcast.67, s32[1,1024]{1,0:T(1,128)S(1)} %get-tuple-element.166.rank_ref, ...), custom_call_target="tpu_custom_call" | custom-call | flops 2147483648 | bytes 20971520 | tf_op jit(solution)/shard_map/cond/branch_1_fun/unpack/pallas_call | solution.py:586
  40.0 0.0 collective-permute-done.b2
  40.0 0.0 collective-permute-done.1.b3
  40.0 0.1 collective-permute-start.5
  40.1 0.5 collective-permute-start.6
  40.6 0.0 collective-permute-done.3.b4
  40.6 0.0 collective-permute-done.4.b5
  40.6 1.2 %collective-permute-done.5.b6 = bf16[4,4,32,384]{3,2,1,0:T(8,128)(2,1)S(1)} collective-permute-done((bf16[4,4,32,384]{3,2,1,0:T(8,128)(2,1)S(1)}, bf16[4,4,32,384]{3,2,1,0:T(8,128)(2,1)S(1)}, u32[]{:S(2)}, u32[]{:S(2)}) %collective-permute-start.5) | collective-permute-done | bytes 393248 | tf_op jit(solution)/shard_map/cond/branch_1_fun/ppermute | solution.py:607
  41.8 0.6 collective-permute-done.6.b7
  42.4 4.0 %cycle.7 = (f32[4,6,32,128]{3,2,1,0:T(8,128)S(1)}, f32[4,6,32,128]{3,2,1,0:T(8,128)S(1)}) custom-call(bf16[4,1024,1024]{2,1,0:T(8,128)(2,1)S(1)} %unpack.3.a_ref, bf16[4,4,32,384]{3,2,1,0:T(8,128)(2,1)} %get-tuple-element.164.b0, bf16[4,4,32,384]{3,2,1,0:T(8,128)(2,1)S(1)} %collective-permute-done.2.b1, bf16[4,4,32,384]{3,2,1,0:T(8,128)(2,1)S(1)} %collective-permute-done.b2, ...), custom_call_target="tpu_custom_call" | custom-call | flops 2147483648 | bytes 14680064 | tf_op jit(solution)/shard_map/cond/branch_1_fun/cycle/pallas_call | solution.py:610
  46.4 2.0 %collective-permute-start.7 = (f32[4,6,32,128]{3,2,1,0:T(8,128)S(1)}, f32[4,6,32,128]{3,2,1,0:T(8,128)S(1)}, u32[]{:S(2)}, u32[]{:S(2)}) collective-permute-start(f32[4,6,32,128]{3,2,1,0:T(8,128)S(1)} %get-tuple-element.172), channel_id=1, source_target_pairs={{0,1},{1,2},{2,3},{3,0},{4,5},{5,6},{6,7},{7,4},{8,9},{9,10},{10,1... | collective-permute-start | bytes 1179656 | tf_op jit(solution)/shard_map/cond/branch_1_fun/ppermute | solution.py:623
  48.4 2.2 %collective-permute-start.9 = (f32[4,6,32,128]{3,2,1,0:T(8,128)S(1)}, f32[4,6,32,128]{3,2,1,0:T(8,128)S(1)}, u32[]{:S(2)}, u32[]{:S(2)}) collective-permute-start(f32[4,6,32,128]{3,2,1,0:T(8,128)S(1)} %get-tuple-element.174), channel_id=1, source_target_pairs={{0,3},{1,0},{2,1},{3,2},{4,7},{5,4},{6,5},{7,6},{8,11},{9,8},{10,9... | collective-permute-start | bytes 1179656 | tf_op jit(solution)/shard_map/cond/branch_1_fun/ppermute | solution.py:623
  50.6 4.0 %cycle.6 = (f32[4,6,32,128]{3,2,1,0:T(8,128)S(1)}, f32[4,6,32,128]{3,2,1,0:T(8,128)S(1)}) custom-call(bf16[4,1024,1024]{2,1,0:T(8,128)(2,1)S(1)} %unpack.3.a_ref, bf16[4,4,32,384]{3,2,1,0:T(8,128)(2,1)} %get-tuple-element.164.b0, bf16[4,4,32,384]{3,2,1,0:T(8,128)(2,1)S(1)} %collective-permute-done.2.b1, bf16[4,4,32,384]{3,2,1,0:T(8,128)(2,1)S(1)} %collective-permute-done.b2, ...), custom_call_target="tpu_custom_call" | custom-call | flops 2147483648 | bytes 14680064 | tf_op jit(solution)/shard_map/cond/branch_1_fun/cycle/pallas_call | solution.py:610
  54.6 0.0 copy-start.1
  54.6 1.9 %collective-permute-start.8 = (f32[4,6,32,128]{3,2,1,0:T(8,128)S(1)}, f32[4,6,32,128]{3,2,1,0:T(8,128)S(1)}, u32[]{:S(2)}, u32[]{:S(2)}) collective-permute-start(f32[4,6,32,128]{3,2,1,0:T(8,128)S(1)} %get-tuple-element.173), channel_id=1, source_target_pairs={{0,2},{1,3},{2,0},{3,1},{4,6},{5,7},{6,4},{7,5},{8,10},{9,11},{10,... | collective-permute-start | bytes 1179656 | tf_op jit(solution)/shard_map/cond/branch_1_fun/ppermute | solution.py:623
  56.5 3.4 %collective-permute-done.7.o1 = f32[4,6,32,128]{3,2,1,0:T(8,128)S(1)} collective-permute-done((f32[4,6,32,128]{3,2,1,0:T(8,128)S(1)}, f32[4,6,32,128]{3,2,1,0:T(8,128)S(1)}, u32[]{:S(2)}, u32[]{:S(2)}) %collective-permute-start.7) | collective-permute-done | bytes 393248 | tf_op jit(solution)/shard_map/cond/branch_1_fun/ppermute | solution.py:623
  59.9 7.8 %collective-permute-done.9.o3 = f32[4,6,32,128]{3,2,1,0:T(8,128)S(1)} collective-permute-done((f32[4,6,32,128]{3,2,1,0:T(8,128)S(1)}, f32[4,6,32,128]{3,2,1,0:T(8,128)S(1)}, u32[]{:S(2)}, u32[]{:S(2)}) %collective-permute-start.9) | collective-permute-done | bytes 393248 | tf_op jit(solution)/shard_map/cond/branch_1_fun/ppermute | solution.py:623
  67.7 1.8 %collective-permute-done.8.o2 = f32[4,6,32,128]{3,2,1,0:T(8,128)S(1)} collective-permute-done((f32[4,6,32,128]{3,2,1,0:T(8,128)S(1)}, f32[4,6,32,128]{3,2,1,0:T(8,128)S(1)}, u32[]{:S(2)}, u32[]{:S(2)}) %collective-permute-start.8) | collective-permute-done | bytes 393248 | tf_op jit(solution)/shard_map/cond/branch_1_fun/ppermute | solution.py:623
  69.5 0.2 sums.3
  69.7 2.3 %collective-permute-start.10 = (f32[6,32,128]{2,1,0:T(8,128)S(1)}, f32[6,32,128]{2,1,0:T(8,128)S(1)}, u32[]{:S(2)}, u32[]{:S(2)}) collective-permute-start(f32[6,32,128]{2,1,0:T(8,128)S(1)} %get-tuple-element.176), channel_id=1, source_target_pairs={{0,24},{4,28},{8,0},{12,4},{16,8},{20,12},{24,16},{28,20},{32,56},... | collective-permute-start | bytes 294920 | tf_op jit(solution)/shard_map/cond/branch_1_fun/ppermute | solution.py:634
  72.1 0.9 %collective-permute-start.11 = (f32[6,32,128]{2,1,0:T(8,128)S(1)}, f32[6,32,128]{2,1,0:T(8,128)S(1)}, u32[]{:S(2)}, u32[]{:S(2)}) collective-permute-start(f32[6,32,128]{2,1,0:T(8,128)S(1)} %get-tuple-element.177), channel_id=1, source_target_pairs={{0,16},{4,20},{8,24},{12,28},{16,0},{20,4},{24,8},{28,12},{32,48},... | collective-permute-start | bytes 294920 | tf_op jit(solution)/shard_map/cond/branch_1_fun/ppermute | solution.py:634
  72.9 0.8 %collective-permute-start.12 = (f32[6,32,128]{2,1,0:T(8,128)S(1)}, f32[6,32,128]{2,1,0:T(8,128)S(1)}, u32[]{:S(2)}, u32[]{:S(2)}) collective-permute-start(f32[6,32,128]{2,1,0:T(8,128)S(1)} %get-tuple-element.178), channel_id=1, source_target_pairs={{0,8},{4,12},{8,16},{12,20},{16,24},{20,28},{24,0},{28,4},{32,40},... | collective-permute-start | bytes 294920 | tf_op jit(solution)/shard_map/cond/branch_1_fun/ppermute | solution.py:634
  73.8 2.1 %collective-permute-done.10.t1 = f32[6,32,128]{2,1,0:T(8,128)S(1)} collective-permute-done((f32[6,32,128]{2,1,0:T(8,128)S(1)}, f32[6,32,128]{2,1,0:T(8,128)S(1)}, u32[]{:S(2)}, u32[]{:S(2)}) %collective-permute-start.10) | collective-permute-done | bytes 98336 | tf_op jit(solution)/shard_map/cond/branch_1_fun/ppermute | solution.py:634
  75.9 2.5 %collective-permute-done.11.t2 = f32[6,32,128]{2,1,0:T(8,128)S(1)} collective-permute-done((f32[6,32,128]{2,1,0:T(8,128)S(1)}, f32[6,32,128]{2,1,0:T(8,128)S(1)}, u32[]{:S(2)}, u32[]{:S(2)}) %collective-permute-start.11) | collective-permute-done | bytes 98336 | tf_op jit(solution)/shard_map/cond/branch_1_fun/ppermute | solution.py:634
  78.4 1.0 %collective-permute-done.12.t3 = f32[6,32,128]{2,1,0:T(8,128)S(1)} collective-permute-done((f32[6,32,128]{2,1,0:T(8,128)S(1)}, f32[6,32,128]{2,1,0:T(8,128)S(1)}, u32[]{:S(2)}, u32[]{:S(2)}) %collective-permute-start.12) | collective-permute-done | bytes 98336 | tf_op jit(solution)/shard_map/cond/branch_1_fun/ppermute | solution.py:634
  79.4 0.0 copy-done.1
  79.4 2.9 %update.3 = f32[8,8,32,256]{3,2,1,0:T(8,128)} custom-call(s32[200]{0:T(256)S(1)} %get-tuple-element.157.occ_ref, s32[8]{0:T(128)S(1)} %get-tuple-element.158.si_ref, s32[8]{0:T(128)S(1)} %get-tuple-element.159.sj_ref, f32[200]{0:T(256)S(1)} %get-tuple-element.160.oe_ref, s32[1,1024]{1,0:T(1,128)S(1)} %bitcast.68, f32[1,1024]{1,0:T(1,128)S(1)} %bitcast.76, ...), custom_call_target="tpu_custom_call" | custom-call | flops 402653184 | bytes 4194304 | tf_op jit(solution)/shard_map/cond/branch_1_fun/update/pallas_call | solution.py:636
Async XLA Ops:
  0.0 9.7 %copy-start.2 = (s32[1024]{0:T(1024)S(1)}, s32[1024]{0:T(1024)}, u32[]{:S(2)}) copy-start(s32[1024]{0:T(1024)} %param.20) | copy-start | bytes 12292
  0.0 9.7 %copy-start.3 = (s32[200]{0:T(256)S(1)}, s32[200]{0:T(256)}, u32[]{:S(2)}) copy-start(s32[200]{0:T(256)} %occ_ref.3) | copy-start | bytes 2404
  0.0 9.7 %copy-start.5 = (s32[4]{0:T(128)S(1)}, s32[4]{0:T(128)}, u32[]{:S(2)}) copy-start(s32[4]{0:T(128)} %sk_ref.3) | copy-start | bytes 52
  0.0 9.7 %copy-start.4 = (s32[8]{0:T(128)S(1)}, s32[8]{0:T(128)}, u32[]{:S(2)}) copy-start(s32[8]{0:T(128)} %si_ref.1) | copy-start | bytes 100
  3.0 10.9 %collective-permute-start.29 = (bf16[4,32,384]{2,1,0:T(8,128)(2,1)S(1)}, bf16[4,32,384]{2,1,0:T(8,128)(2,1)S(1)}, u32[]{:S(2)}, u32[]{:S(2)}) collective-permute-start(bf16[4,32,384]{2,1,0:T(8,128)(2,1)S(1)} %get-tuple-element.189), channel_id=1, source_target_pairs={{0,8},{4,12},{8,16},{12,20},{16,24},{20,28},{24,0},{28,4},{32,40},... | collective-permute-start | bytes 294920 | tf_op jit(solution)/shard_map/ppermute | solution.py:551
  4.8 9.2 %collective-permute-start.30 = (bf16[4,32,384]{2,1,0:T(8,128)(2,1)S(1)}, bf16[4,32,384]{2,1,0:T(8,128)(2,1)S(1)}, u32[]{:S(2)}, u32[]{:S(2)}) collective-permute-start(bf16[4,32,384]{2,1,0:T(8,128)(2,1)S(1)} %get-tuple-element.190), channel_id=1, source_target_pairs={{0,16},{4,20},{8,24},{12,28},{16,0},{20,4},{24,8},{28,12},{32,48},... | collective-permute-start | bytes 294920 | tf_op jit(solution)/shard_map/ppermute | solution.py:551
  7.7 6.3 %collective-permute-start.31 = (bf16[4,32,384]{2,1,0:T(8,128)(2,1)S(1)}, bf16[4,32,384]{2,1,0:T(8,128)(2,1)S(1)}, u32[]{:S(2)}, u32[]{:S(2)}) collective-permute-start(bf16[4,32,384]{2,1,0:T(8,128)(2,1)S(1)} %get-tuple-element.191), channel_id=1, source_target_pairs={{0,24},{4,28},{8,0},{12,4},{16,8},{20,12},{24,16},{28,20},{32,56},... | collective-permute-start | bytes 294920 | tf_op jit(solution)/shard_map/ppermute | solution.py:551
  9.7 5.0 %copy-start.6 = (f32[1024]{0:T(1024)S(1)}, f32[1024]{0:T(1024)}, u32[]{:S(2)}) copy-start(f32[1024]{0:T(1024)} %param.22) | copy-start | bytes 12292
  9.8 5.0 %copy-start.7 = (s32[8]{0:T(128)S(1)}, s32[8]{0:T(128)}, u32[]{:S(2)}) copy-start(s32[8]{0:T(128)} %sj_ref.1) | copy-start | bytes 100
  9.8 5.0 %copy-start.8 = (f32[200]{0:T(256)S(1)}, f32[200]{0:T(256)}, u32[]{:S(2)}) copy-start(f32[200]{0:T(256)} %param.21) | copy-start | bytes 2404
  15.0 20.9 %all-to-all-start = ((bf16[4,4,10,32,128]{4,3,2,1,0:T(8,128)(2,1)}), bf16[4,4,10,32,128]{4,3,2,1,0:T(8,128)(2,1)S(1)}, u32[]{:S(2)}, u32[]{:S(2)}) async-start(bf16[4,4,10,32,128]{4,3,2,1,0:T(8,128)(2,1)} %get-tuple-element.167), calls=%async_computation | async-start | bytes 2621440 | tf_op jit(solution)/shard_map/cond/branch_1_fun/all_to_all | solution.py:583
  18.6 12.5 %collective-permute-start.2 = (bf16[4,4,32,384]{3,2,1,0:T(8,128)(2,1)}, bf16[4,4,32,384]{3,2,1,0:T(8,128)(2,1)S(1)}, u32[]{:S(2)}, u32[]{:S(2)}) collective-permute-start(bf16[4,4,32,384]{3,2,1,0:T(8,128)(2,1)} %get-tuple-element.164.b0), channel_id=1, source_target_pairs={{0,32},{4,36},{8,40},{12,44},{16,48},{20,52},{24,56},{28,60},{32,6... | collective-permute-start | bytes 1179656 | tf_op jit(solution)/shard_map/cond/branch_1_fun/ppermute | solution.py:605
  20.2 19.9 %collective-permute-start = (bf16[4,4,32,384]{3,2,1,0:T(8,128)(2,1)}, bf16[4,4,32,384]{3,2,1,0:T(8,128)(2,1)S(1)}, u32[]{:S(2)}, u32[]{:S(2)}) collective-permute-start(bf16[4,4,32,384]{3,2,1,0:T(8,128)(2,1)} %get-tuple-element.164.b0), channel_id=1, source_target_pairs={{0,64},{4,68},{8,72},{12,76},{16,80},{20,84},{24,88},{28,92},{32,9... | collective-permute-start | bytes 1179656 | tf_op jit(solution)/shard_map/cond/branch_1_fun/ppermute | solution.py:605
  22.9 17.1 %collective-permute-start.1 = (bf16[4,4,32,384]{3,2,1,0:T(8,128)(2,1)}, bf16[4,4,32,384]{3,2,1,0:T(8,128)(2,1)S(1)}, u32[]{:S(2)}, u32[]{:S(2)}) collective-permute-start(bf16[4,4,32,384]{3,2,1,0:T(8,128)(2,1)} %get-tuple-element.164.b0), channel_id=1, source_target_pairs={{0,96},{4,100},{8,104},{12,108},{16,112},{20,116},{24,120},{28,124... | collective-permute-start | bytes 1179656 | tf_op jit(solution)/shard_map/cond/branch_1_fun/ppermute | solution.py:605
  24.3 16.3 %collective-permute-start.3 = (bf16[4,4,32,384]{3,2,1,0:T(8,128)(2,1)}, bf16[4,4,32,384]{3,2,1,0:T(8,128)(2,1)S(1)}, u32[]{:S(2)}, u32[]{:S(2)}) collective-permute-start(bf16[4,4,32,384]{3,2,1,0:T(8,128)(2,1)} %get-tuple-element.164.b0), channel_id=1, source_target_pairs={{0,4},{4,0},{8,12},{12,8},{16,20},{20,16},{24,28},{28,24},{32,36},... | collective-permute-start | bytes 1179656 | tf_op jit(solution)/shard_map/cond/branch_1_fun/ppermute | solution.py:607
  31.1 9.5 %collective-permute-start.4 = (bf16[4,4,32,384]{3,2,1,0:T(8,128)(2,1)S(1)}, bf16[4,4,32,384]{3,2,1,0:T(8,128)(2,1)S(1)}, u32[]{:S(2)}, u32[]{:S(2)}) collective-permute-start(bf16[4,4,32,384]{3,2,1,0:T(8,128)(2,1)S(1)} %collective-permute-done.2.b1), channel_id=1, source_target_pairs={{0,4},{4,0},{8,12},{12,8},{16,20},{20,16},{24,28},{28,24},{32,36},... | collective-permute-start | bytes 1179656 | tf_op jit(solution)/shard_map/cond/branch_1_fun/ppermute | solution.py:607
  40.0 1.8 %collective-permute-start.5 = (bf16[4,4,32,384]{3,2,1,0:T(8,128)(2,1)S(1)}, bf16[4,4,32,384]{3,2,1,0:T(8,128)(2,1)S(1)}, u32[]{:S(2)}, u32[]{:S(2)}) collective-permute-start(bf16[4,4,32,384]{3,2,1,0:T(8,128)(2,1)S(1)} %collective-permute-done.b2), channel_id=1, source_target_pairs={{0,4},{4,0},{8,12},{12,8},{16,20},{20,16},{24,28},{28,24},{32,36},... | collective-permute-start | bytes 1179656 | tf_op jit(solution)/shard_map/cond/branch_1_fun/ppermute | solution.py:607
  40.1 2.3 %collective-permute-start.6 = (bf16[4,4,32,384]{3,2,1,0:T(8,128)(2,1)S(1)}, bf16[4,4,32,384]{3,2,1,0:T(8,128)(2,1)S(1)}, u32[]{:S(2)}, u32[]{:S(2)}) collective-permute-start(bf16[4,4,32,384]{3,2,1,0:T(8,128)(2,1)S(1)} %collective-permute-done.1.b3), channel_id=1, source_target_pairs={{0,4},{4,0},{8,12},{12,8},{16,20},{20,16},{24,28},{28,24},{32,36},... | collective-permute-start | bytes 1179656 | tf_op jit(solution)/shard_map/cond/branch_1_fun/ppermute | solution.py:607
  46.4 13.5 %collective-permute-start.7 = (f32[4,6,32,128]{3,2,1,0:T(8,128)S(1)}, f32[4,6,32,128]{3,2,1,0:T(8,128)S(1)}, u32[]{:S(2)}, u32[]{:S(2)}) collective-permute-start(f32[4,6,32,128]{3,2,1,0:T(8,128)S(1)} %get-tuple-element.172), channel_id=1, source_target_pairs={{0,1},{1,2},{2,3},{3,0},{4,5},{5,6},{6,7},{7,4},{8,9},{9,10},{10,1... | collective-permute-start | bytes 1179656 | tf_op jit(solution)/shard_map/cond/branch_1_fun/ppermute | solution.py:623
  48.4 19.3 %collective-permute-start.9 = (f32[4,6,32,128]{3,2,1,0:T(8,128)S(1)}, f32[4,6,32,128]{3,2,1,0:T(8,128)S(1)}, u32[]{:S(2)}, u32[]{:S(2)}) collective-permute-start(f32[4,6,32,128]{3,2,1,0:T(8,128)S(1)} %get-tuple-element.174), channel_id=1, source_target_pairs={{0,3},{1,0},{2,1},{3,2},{4,7},{5,4},{6,5},{7,6},{8,11},{9,8},{10,9... | collective-permute-start | bytes 1179656 | tf_op jit(solution)/shard_map/cond/branch_1_fun/ppermute | solution.py:623
  54.6 24.8 %copy-start.1 = (bf16[8,8,32,256]{3,2,1,0:T(8,128)(2,1)S(1)}, bf16[8,8,32,256]{3,2,1,0:T(8,128)(2,1)}, u32[]{:S(2)}) copy-start(bf16[8,8,32,256]{3,2,1,0:T(8,128)(2,1)} %get-tuple-element.179.int_ref) | copy-start | bytes 3145732 | tf_op jit(solution)/shard_map/cond
  54.6 14.9 %collective-permute-start.8 = (f32[4,6,32,128]{3,2,1,0:T(8,128)S(1)}, f32[4,6,32,128]{3,2,1,0:T(8,128)S(1)}, u32[]{:S(2)}, u32[]{:S(2)}) collective-permute-start(f32[4,6,32,128]{3,2,1,0:T(8,128)S(1)} %get-tuple-element.173), channel_id=1, source_target_pairs={{0,2},{1,3},{2,0},{3,1},{4,6},{5,7},{6,4},{7,5},{8,10},{9,11},{10,... | collective-permute-start | bytes 1179656 | tf_op jit(solution)/shard_map/cond/branch_1_fun/ppermute | solution.py:623
  69.7 6.2 %collective-permute-start.10 = (f32[6,32,128]{2,1,0:T(8,128)S(1)}, f32[6,32,128]{2,1,0:T(8,128)S(1)}, u32[]{:S(2)}, u32[]{:S(2)}) collective-permute-start(f32[6,32,128]{2,1,0:T(8,128)S(1)} %get-tuple-element.176), channel_id=1, source_target_pairs={{0,24},{4,28},{8,0},{12,4},{16,8},{20,12},{24,16},{28,20},{32,56},... | collective-permute-start | bytes 294920 | tf_op jit(solution)/shard_map/cond/branch_1_fun/ppermute | solution.py:634
  72.1 6.4 %collective-permute-start.11 = (f32[6,32,128]{2,1,0:T(8,128)S(1)}, f32[6,32,128]{2,1,0:T(8,128)S(1)}, u32[]{:S(2)}, u32[]{:S(2)}) collective-permute-start(f32[6,32,128]{2,1,0:T(8,128)S(1)} %get-tuple-element.177), channel_id=1, source_target_pairs={{0,16},{4,20},{8,24},{12,28},{16,0},{20,4},{24,8},{28,12},{32,48},... | collective-permute-start | bytes 294920 | tf_op jit(solution)/shard_map/cond/branch_1_fun/ppermute | solution.py:634
  72.9 6.5 %collective-permute-start.12 = (f32[6,32,128]{2,1,0:T(8,128)S(1)}, f32[6,32,128]{2,1,0:T(8,128)S(1)}, u32[]{:S(2)}, u32[]{:S(2)}) collective-permute-start(f32[6,32,128]{2,1,0:T(8,128)S(1)} %get-tuple-element.178), channel_id=1, source_target_pairs={{0,8},{4,12},{8,16},{12,20},{16,24},{20,28},{24,0},{28,4},{32,40},... | collective-permute-start | bytes 294920 | tf_op jit(solution)/shard_map/cond/branch_1_fun/ppermute | solution.py:634
